TPU v7x, 512 devices: a whole 4x4x16 slice. The times are simulated.
512 devices in a mesh: blk: 128 (over z_lo, y, x), freq: 4 (over z_hi, core).
Axes of the slice: x: 4, y: 4, z: 16 (z_hi: 2, z_lo: 8; z = z_hi * 8 + z_lo), core: 2. Of those that a mesh axis runs over, the one named last changes fastest.
Arguments:
- samples: bfloat16 [1024, 64, 2048], P('blk', 'freq'), may hold values from -6 to 6
- channel_lists: int32 [4, 128, 2], replicated, may hold values from 0 to 1023, as said below
- channel_counts: int32 [4, 128], P('freq', 'blk'), may hold values from 0 to 2, as said below
Outputs:
- visibilities: bfloat16 [4, 128, 2, 136, 2, 4096], P('freq', 'blk')
Inputs may be any that keep to these rules, and one draw needn't show every extreme that they name: `channel_lists`: the slots of owner (f, b) hold channels of the f-th quarter, f * 256 to (f + 1) * 256 - 1, distinct within one owner; only the first channel_counts[f, b] slots are live. `channel_counts`: in every quarter some owner has all 2 slots live.
All inputs are finite; a program needn't handle non-finite values.
Results may differ from a plain program's by a relative error of at most 0.0078.
Values may be sent and summed in bfloat16 or wider, within the bound.
No kernel may reach another device: no remote copies, remote signals or barrier semaphores. Data moves between devices by JAX's collectives and lax.ppermute only.
A program may use at most 128 MiB of HBM per device.

v0:
```python
import math

import jax
import jax.numpy as jnp
import ml_dtypes
import numpy as np
from jax import lax
from jax.experimental import pallas as pl
from jax.experimental.pallas import tpu as pltpu
from jax.sharding import PartitionSpec as P

FRAME = 2048
HALF = 1024
TAPS = 16
INS = 8
OUT_T = 24
COLS = INS * OUT_T
LANES = 2 * COLS
QUARTER = 256
N_BLK = 128
N_FREQ = 4
TILES = 16
PAIRS = 136
GROUPS = ((0, 2), (0, 2), (0, 1, 2), (1,))


def window_taps():
    total_len = FRAME * TAPS
    m = np.arange(total_len, dtype=np.float64)
    shaped = np.sinc((m - total_len / 2 + 0.5) / FRAME)
    shaped = shaped * (0.5 - 0.5 * np.cos(2.0 * np.pi * (m + 0.5) / total_len))
    shaped = shaped / np.sqrt(np.sum(shaped * shaped) / FRAME)
    return shaped.reshape(TAPS, FRAME).astype(np.float32)


def fourier_halves():
    channels = np.arange(1024).reshape(4, 128, 2).transpose(0, 2, 1)
    phase = channels[..., None] * np.arange(HALF) % FRAME
    angle = phase * (2.0 * np.pi / FRAME)
    scale = 1.0 / math.sqrt(FRAME)
    both = np.concatenate([np.cos(angle) * scale, -np.sin(angle) * scale], axis=2)
    return both.astype(np.float32).astype(ml_dtypes.bfloat16)


def message_lane(r, col):
    if col < 128:
        return 256 * r + col
    return 128 + 64 * r + col - 128


def merge_matrices():
    blocks = []
    for pair, tiles in enumerate(GROUPS):
        block = np.zeros((N_FREQ, len(tiles), 128, 2, 128), np.float32)
        for f in range(N_FREQ):
            for h in range(2):
                for t in range(OUT_T):
                    local = OUT_T * (f % 2) + t
                    if local > 46:
                        continue
                    spectrum = (32 * (f // 2) + local) % 64
                    for r in range(2):
                        lane = message_lane(r, (2 * pair + h) * OUT_T + t)
                        block[f, tiles.index(lane // 128), lane % 128, h, r * 64 + spectrum] = 1.0
        blocks.append(block.reshape(-1, 256))
    return np.concatenate(blocks).astype(ml_dtypes.bfloat16)


def nt_dot(a, b):
    return lax.dot_general(a, b, (((1,), (1,)), ((), ())), preferred_element_type=jnp.float32)


def channel_kernel(core_ref, own_ref, other_ref, window_ref, table_ref, list_ref, out_ref, u_ref, v_ref):
    step = pl.program_id(0)

    @pl.when(step == 0)
    def _():
        second = core_ref[0] == 1
        width = 256
        u_ref[COLS:, :] = jnp.zeros((256 - COLS, HALF), jnp.bfloat16)
        v_ref[COLS:, :] = jnp.zeros((256 - COLS, HALF), jnp.bfloat16)

        def filtered(i, start):
            lanes = pl.ds(pl.multiple_of(start, width), width)
            own = own_ref[i, :, lanes].astype(jnp.float32)
            other = other_ref[i, :, lanes].astype(jnp.float32)
            zero = jnp.zeros((8, width), jnp.float32)
            extended = jnp.concatenate(
                [
                    jnp.where(second, other[8:], zero),
                    jnp.where(second, own[:8], zero),
                    jnp.where(second, own[8:], own[:8]),
                    jnp.where(second, zero, own[8:]),
                    jnp.where(second, zero, other[:8]),
                ],
                axis=0,
            )
            total = window_ref[7:8, lanes] * extended[8:32] + window_ref[15:16, lanes] * extended[16:40]
            for by in range(1, 8):
                moved = extended[by : by + 32]
                total = total + window_ref[by - 1 : by, lanes] * moved[0:24]
                total = total + window_ref[by + 7 : by + 8, lanes] * moved[8:32]
            return total

        def one(index, carry):
            pair = index // (HALF // width)
            start = (index % (HALF // width)) * width
            rows = pl.ds(pl.multiple_of(pair * 48, 16), 48)
            lanes = pl.ds(pl.multiple_of(start, width), width)
            low = [filtered(2 * pair + h, start) for h in range(2)]
            high = [filtered(2 * pair + h, start + HALF) for h in range(2)]
            low = jnp.concatenate(low, axis=0)
            high = jnp.concatenate(high, axis=0)
            u_ref[rows, lanes] = (low + high).astype(jnp.bfloat16)
            v_ref[rows, lanes] = (low - high).astype(jnp.bfloat16)
            return carry

        lax.fori_loop(0, (INS // 2) * (HALF // width), one, 0)

    halves = []
    for parity, folded in enumerate((u_ref, v_ref)):
        y = nt_dot(table_ref[0, parity], folded[...])
        middle = y[:128, 128:] + pltpu.roll(y[128:, 128:], 64, 1)
        halves.append(jnp.concatenate([y[:128, :128], middle, y[128:, :128]], axis=1))
    spectra = jnp.concatenate(halves, axis=0).astype(jnp.bfloat16)
    channels = list_ref[0]
    place = (channels & 1) * 128 + ((channels & 255) >> 1)
    picks = (lax.broadcasted_iota(jnp.int32, (QUARTER, QUARTER), 0) == place).astype(jnp.float32)
    out_ref[...] = jnp.dot(
        picks.T.astype(jnp.bfloat16), spectra, preferred_element_type=jnp.float32
    ).astype(jnp.bfloat16)


def channel_messages(core, own, other, lists):
    window = jnp.asarray(window_taps())
    table = jnp.asarray(fourier_halves())
    return pl.pallas_call(
        channel_kernel,
        grid=(N_FREQ,),
        in_specs=[
            pl.BlockSpec(memory_space=pltpu.SMEM),
            pl.BlockSpec((INS, 16, FRAME), lambda q: (0, 0, 0)),
            pl.BlockSpec((INS, 16, FRAME), lambda q: (0, 0, 0)),
            pl.BlockSpec((TAPS, FRAME), lambda q: (0, 0)),
            pl.BlockSpec((1, 2, 256, HALF), lambda q: (q, 0, 0, 0)),
            pl.BlockSpec((1, 1, QUARTER), lambda q: (q, 0, 0)),
        ],
        out_specs=pl.BlockSpec((QUARTER, LANES), lambda q: (q, 0)),
        out_shape=jax.ShapeDtypeStruct((N_FREQ * QUARTER, LANES), jnp.bfloat16),
        scratch_shapes=[pltpu.VMEM((256, HALF), jnp.bfloat16), pltpu.VMEM((256, HALF), jnp.bfloat16)],
        compiler_params=pltpu.CompilerParams(vmem_limit_bytes=40 << 20),
        name="channels",
    )(core, own, other, window, table, lists)


def correlate_kernel(count_ref, got_ref, merge_ref, out_ref, right_all, even_all, odd_all, left_ref, right_ref):
    slot = pl.program_id(0)

    @pl.when(slot == 0)
    def _():
        sign = jnp.where(lax.broadcasted_iota(jnp.int32, (1, 128), 1) < 64, 1.0, -1.0)
        base = 0
        for pair, tiles in enumerate(GROUPS):
            depth = N_FREQ * len(tiles) * 128
            parts = [
                got_ref[f * 256 : (f + 1) * 256, tile * 128 : (tile + 1) * 128]
                for f in range(N_FREQ)
                for tile in tiles
            ]
            both = jnp.dot(
                jnp.concatenate(parts, axis=1),
                merge_ref[base : base + depth, :],
                preferred_element_type=jnp.float32,
            )
            base += depth
            for h in range(2):
                plain = both[:, h * 128 : (h + 1) * 128]
                turned = pltpu.roll(plain, 64, 1) * sign
                right_all[pl.ds(2 * pair + h, 256, stride=8), :] = plain
                left_all = (even_all, odd_all)[h]
                left_all[pl.ds(2 * pair, 256, stride=8), :] = plain
                left_all[pl.ds(2 * pair + 1, 256, stride=8), :] = turned

    live = slot < count_ref[0, 0]

    @pl.when(live)
    def _():
        def tile_of(ref, tile):
            return jnp.concatenate(
                [
                    ref[pl.ds(pl.multiple_of((tile * 8 + b) * 16 + slot * 8, 8), 8), :]
                    for b in range(8)
                ],
                axis=0,
            ).astype(jnp.bfloat16)

        for tile in range(TILES):
            rows = slice(tile * 64, tile * 64 + 64)
            left_ref[rows, :128] = tile_of(even_all, tile)
            left_ref[rows, 128:] = tile_of(odd_all, tile)
            right_ref[rows, :] = tile_of(right_all, tile)
        zero = jnp.zeros((64, 128), jnp.bfloat16)
        for m in range(TILES // 2):
            rhs = []
            for q in (2 * m, 2 * m + 1):
                column = right_ref[q * 64 : (q + 1) * 64, :]
                rhs.append(jnp.concatenate([column, zero], axis=1))
                rhs.append(jnp.concatenate([zero, column], axis=1))
            products = nt_dot(left_ref[: (2 * m + 2) * 64, :], jnp.concatenate(rhs, axis=0))
            for h in range(2):
                q = 2 * m + h
                for p in range(q + 1):
                    t = TILES * p - p * (p - 1) // 2 + q - p
                    piece = products[p * 64 : (p + 1) * 64, h * 128 : (h + 1) * 128]
                    out_ref[0, t] = (piece * (1.0 / 64.0)).astype(jnp.bfloat16)

    @pl.when(jnp.logical_not(live))
    def _():
        out_ref[...] = jnp.zeros(out_ref.shape, out_ref.dtype)


def visibility_tiles(counts, got):
    merge = jnp.asarray(merge_matrices())
    return pl.pallas_call(
        correlate_kernel,
        grid=(2,),
        in_specs=[
            pl.BlockSpec(memory_space=pltpu.SMEM),
            pl.BlockSpec((1024, LANES), lambda j: (0, 0)),
            pl.BlockSpec(merge.shape, lambda j: (0, 0)),
        ],
        out_specs=pl.BlockSpec((1, PAIRS, 64, 128), lambda j: (j, 0, 0, 0)),
        out_shape=jax.ShapeDtypeStruct((2, PAIRS, 64, 128), jnp.bfloat16),
        scratch_shapes=[
            pltpu.VMEM((2048, 128), jnp.float32),
            pltpu.VMEM((2048, 128), jnp.float32),
            pltpu.VMEM((2048, 128), jnp.float32),
            pltpu.VMEM((1024, 256), jnp.bfloat16),
            pltpu.VMEM((1024, 128), jnp.bfloat16),
        ],
        compiler_params=pltpu.CompilerParams(vmem_limit_bytes=40 << 20),
        name="correlate",
    )(counts, got, merge)


def shards(samples, channel_lists, channel_counts):
    freq = lax.axis_index("freq")
    core = (freq % 2).astype(jnp.int32).reshape(1)
    other = lax.ppermute(samples, "freq", [(i, i ^ 1) for i in range(N_FREQ)])
    lists = channel_lists.reshape(N_FREQ, 1, QUARTER)
    messages = channel_messages(core, samples, other, lists)
    got = lax.all_to_all(
        messages.reshape(N_FREQ * N_BLK, 2, LANES), ("freq", "blk"), 0, 0, tiled=True
    ).reshape(1024, LANES)
    tiles = visibility_tiles(channel_counts, got)
    tiles = tiles.reshape(2, PAIRS, 32, 2, 128).transpose(0, 1, 3, 2, 4)
    return tiles.reshape(1, 1, 2, PAIRS, 2, 4096)


def solution(mesh):
    in_specs = (P("blk", "freq", None), P(), P("freq", "blk"))
    out_specs = P("freq", "blk", None, None, None, None)
    return jax.shard_map(shards, mesh=mesh, in_specs=in_specs, out_specs=out_specs, check_vma=False)
```

profile of v0, /device:TPU:1, one launch (start us, length us, event | category | flops | bytes accessed | tf_op | source)
XLA Modules:
  0.0 94.0 jit_solution(6066186775694387906)
XLA Ops:
  0.0 8.8 %collective-permute-start = (bf16[8,16,2048]{2,1,0:T(8,128)(2,1)}, bf16[8,16,2048]{2,1,0:T(8,128)(2,1)S(1)}, u32[]{:S(2)}, u32[]{:S(2)}) collective-permute-start(bf16[8,16,2048]{2,1,0:T(8,128)(2,1)} %own_ref.1), channel_id=1, source_target_pairs={{0,1},{1,0},{2,3},{3,2},{4,5},{5,4},{6,7},{7,6},{8,9},{9,8},{10,11... | collective-permute-start | bytes 1572872 | tf_op jit(solution)/shard_map/ppermute | solution.py:249
  8.8 0.8 copy.9
  9.6 0.1 copy.10.list_ref
  9.7 0.8 collective-permute-done.other_ref
  10.5 0.0 copy-start
  10.5 2.2 %copy-done = bf16[4,2,256,1024]{3,2,1,0:T(8,128)(2,1)S(1)} copy-done((bf16[4,2,256,1024]{3,2,1,0:T(8,128)(2,1)S(1)}, bf16[4,2,256,1024]{3,2,1,0:T(8,128)(2,1)}, u32[]{:S(2)}) %copy-start) | copy-done | bytes 4194328
  12.7 0.0 copy-start.2
  12.7 1.0 %copy-done.2 = bf16[8,16,2048]{2,1,0:T(8,128)(2,1)S(1)} copy-done((bf16[8,16,2048]{2,1,0:T(8,128)(2,1)S(1)}, bf16[8,16,2048]{2,1,0:T(8,128)(2,1)}, u32[]{:S(2)}) %copy-start.2) | copy-done | bytes 524312
  13.7 0.0 copy-start.3
  13.7 0.9 copy-done.3
  14.6 0.0 copy-start.1
  14.6 7.6 %channels.1 = bf16[1024,384]{1,0:T(8,128)(2,1)S(1)} custom-call(s32[1]{0:T(128)} %bitcast.core_ref, bf16[8,16,2048]{2,1,0:T(8,128)(2,1)S(1)} %copy-done.2, bf16[8,16,2048]{2,1,0:T(8,128)(2,1)S(1)} %collective-permute-done.other_ref, f32[16,2048]{1,0:T(8,128)S(1)} %copy-done.3, bf16[4,2,256,1024]{3,2,1,0:T(8,128)(2,1)S(1)} %copy-done, ...), custom_call_target="tpu_custom_call" | custom-call | tf_op jit(solution)/shard_map/channels/pallas_call | solution.py:137
  22.2 1.2 %reshape.20 = bf16[512,2,384]{2,1,0:T(2,128)(2,1)} reshape(bf16[1024,384]{1,0:T(8,128)(2,1)S(1)} %channels.1) | data formatting | bytes 1572864 | tf_op jit(solution)/shard_map/reshape | solution.py:253
  23.4 19.6 %all-to-all-start = ((bf16[512,2,384]{2,1,0:T(2,128)(2,1)}), bf16[512,2,384]{2,1,0:T(2,128)(2,1)}, u32[]{:S(2)}, u32[]{:S(2)}) async-start(bf16[512,2,384]{2,1,0:T(2,128)(2,1)} %reshape.20), calls=%async_computation | async-start | bytes 1572864 | tf_op jit(solution)/shard_map/all_to_all | solution.py:252
  43.7 44.6 %all-to-all-done = bf16[512,2,384]{2,1,0:T(2,128)(2,1)} async-done(((bf16[512,2,384]{2,1,0:T(2,128)(2,1)}), bf16[512,2,384]{2,1,0:T(2,128)(2,1)}, u32[]{:S(2)}, u32[]{:S(2)}) %all-to-all-start) | async-done | bytes 786464 | tf_op jit(solution)/shard_map/all_to_all | solution.py:252
  88.3 2.3 %reshape.21.got_ref = bf16[1024,384]{1,0:T(8,128)(2,1)S(1)} reshape(bf16[512,2,384]{2,1,0:T(2,128)(2,1)} %all-to-all-done) | data formatting | bytes 1572864 | tf_op jit(solution)/shard_map/reshape | solution.py:254
  90.5 0.0 copy-done.1
  90.5 3.5 %correlate.1 = bf16[2,136,64,128]{3,2,1,0:T(8,128)(2,1)} custom-call(s32[1,1]{1,0:T(1,128)S(6)} %copy.12.count_ref, bf16[1024,384]{1,0:T(8,128)(2,1)S(1)} %reshape.21.got_ref, bf16[4096,256]{1,0:T(8,128)(2,1)S(1)} %copy-done.1), custom_call_target="tpu_custom_call" | custom-call | tf_op jit(solution)/shard_map/correlate/pallas_call | solution.py:224
Async XLA Ops:
  0.0 10.5 %collective-permute-start = (bf16[8,16,2048]{2,1,0:T(8,128)(2,1)}, bf16[8,16,2048]{2,1,0:T(8,128)(2,1)S(1)}, u32[]{:S(2)}, u32[]{:S(2)}) collective-permute-start(bf16[8,16,2048]{2,1,0:T(8,128)(2,1)} %own_ref.1), channel_id=1, source_target_pairs={{0,1},{1,0},{2,3},{3,2},{4,5},{5,4},{6,7},{7,6},{8,9},{9,8},{10,11... | collective-permute-start | bytes 1572872 | tf_op jit(solution)/shard_map/ppermute | solution.py:249
  10.5 2.2 %copy-start = (bf16[4,2,256,1024]{3,2,1,0:T(8,128)(2,1)S(1)}, bf16[4,2,256,1024]{3,2,1,0:T(8,128)(2,1)}, u32[]{:S(2)}) copy-start(bf16[4,2,256,1024]{3,2,1,0:T(8,128)(2,1)} %constant.24.clone.table_ref) | copy-start | bytes 12582916
  12.7 1.0 %copy-start.2 = (bf16[8,16,2048]{2,1,0:T(8,128)(2,1)S(1)}, bf16[8,16,2048]{2,1,0:T(8,128)(2,1)}, u32[]{:S(2)}) copy-start(bf16[8,16,2048]{2,1,0:T(8,128)(2,1)} %own_ref.1) | copy-start | bytes 1572868
  13.7 0.9 copy-start.3
  14.6 75.9 %copy-start.1 = (bf16[4096,256]{1,0:T(8,128)(2,1)S(1)}, bf16[4096,256]{1,0:T(8,128)(2,1)}, u32[]{:S(2)}) copy-start(bf16[4096,256]{1,0:T(8,128)(2,1)} %constant.25.clone.merge_ref) | copy-start | bytes 6291460
  23.4 64.8 %all-to-all-start = ((bf16[512,2,384]{2,1,0:T(2,128)(2,1)}), bf16[512,2,384]{2,1,0:T(2,128)(2,1)}, u32[]{:S(2)}, u32[]{:S(2)}) async-start(bf16[512,2,384]{2,1,0:T(2,128)(2,1)} %reshape.20), calls=%async_computation | async-start | bytes 1572864 | tf_op jit(solution)/shard_map/all_to_all | solution.py:252
where the time goes:
time: 94.3 us; the launch traced here: 94 us
  waiting for transfers between devices  45.4 us (48%)
  starting transfers between devices  28.4 us (30%)
  Pallas kernels  11 us (12%)
  local copies, waits for them, and re-layouts  8.48 us (9%)
    all_to_all x1, waiting for transfers between devices, shards(): lax.all_to_all(messages.reshape(N_FREQ * N_BLK, 2, LANES), ('freq', 'blk'...  44.6 us
    all_to_all x1, starting transfers between devices, shards(): lax.all_to_all(messages.reshape(N_FREQ * N_BLK, 2, LANES), ('freq', 'blk'...  19.6 us
    ppermute x1, starting transfers between devices, shards(): other = lax.ppermute(samples, 'freq', [(i, i ^ 1) for i in range(N_FREQ)])  8.78 us
    pallas_call x1, Pallas kernels, channel_messages(): pl.pallas_call(channel_kernel, grid=(N_FREQ,), in_specs=[pl.BlockSpec(mem...  7.57 us
    unnamed x9, local copies, waits for them, and re-layouts  4.97 us
    pallas_call x1, Pallas kernels, visibility_tiles(): pl.pallas_call(correlate_kernel, grid=(2,), in_specs=[pl.BlockSpec(memory...  3.46 us
    reshape x1, local copies, waits for them, and re-layouts, shards(): got = lax.all_to_all(messages.reshape(N_FREQ * N_BLK, 2, LANES), ('freq',...  2.26 us
  transfers between devices with their start and end apart: 2, of which 2 were waited for; matrix products, arithmetic and copies ran while one was open for 1% of the time, Pallas kernels for 0%

commit v1 on v0

v1 whole, which is shorter than its diff:
```python
import math

import jax
import jax.numpy as jnp
import ml_dtypes
import numpy as np
from jax import lax
from jax.experimental import pallas as pl
from jax.experimental.pallas import tpu as pltpu
from jax.sharding import Mesh, PartitionSpec as P

FRAME = 2048
HALF = 1024
TAPS = 16
INS = 8
OUT_T = 24
QUARTER = 256
N_BLK = 128
N_FREQ = 4
TILES = 16
PAIRS = 136
GROUPS = ((0, 1), (0, 1), (1, 2), (1, 2))


def window_taps():
    total_len = FRAME * TAPS
    m = np.arange(total_len, dtype=np.float64)
    shaped = np.sinc((m - total_len / 2 + 0.5) / FRAME)
    shaped = shaped * (0.5 - 0.5 * np.cos(2.0 * np.pi * (m + 0.5) / total_len))
    shaped = shaped / np.sqrt(np.sum(shaped * shaped) / FRAME)
    return shaped.reshape(TAPS, FRAME).astype(np.float32)


def fourier_halves():
    channels = np.arange(1024).reshape(4, 128, 2).transpose(0, 2, 1)
    phase = channels[..., None] * np.arange(HALF) % FRAME
    angle = phase * (2.0 * np.pi / FRAME)
    scale = 1.0 / math.sqrt(FRAME)
    both = np.concatenate([np.cos(angle) * scale, -np.sin(angle) * scale], axis=2)
    return both.astype(np.float32).astype(ml_dtypes.bfloat16)


def message_lane(core, i, t, r):
    if 16 * core <= 2 * t < 32 + 16 * core:
        return i // 4 * 256 + 64 * r + i % 4 * 16 + t - 8 * core
    return 128 + 64 * r + i * 8 + t % 8


def merge_matrices():
    blocks = []
    for pair, tiles in enumerate(GROUPS):
        block = np.zeros((N_FREQ, len(tiles), 128, 2, 128), np.float32)
        for f in range(N_FREQ):
            for h in range(2):
                for t in range(OUT_T):
                    local = OUT_T * (f % 2) + t
                    if local > 46:
                        continue
                    spectrum = (32 * (f // 2) + local) % 64
                    for r in range(2):
                        lane = message_lane(f % 2, 2 * pair + h, t, r)
                        block[f, tiles.index(lane // 128), lane % 128, h, r * 64 + spectrum] = 1.0
        blocks.append(block.reshape(-1, 256))
    return np.concatenate(blocks).astype(ml_dtypes.bfloat16)


def nt_dot(a, b):
    return lax.dot_general(a, b, (((1,), (1,)), ((), ())), preferred_element_type=jnp.float32)


def filtered(extended, window_ref, lanes):
    count = extended.shape[0] - 16
    total = window_ref[7:8, lanes] * extended[8 : 8 + count] + window_ref[15:16, lanes] * extended[16:]
    for by in range(1, 8):
        moved = extended[by : by + count + 8]
        total = total + window_ref[by - 1 : by, lanes] * moved[:count]
        total = total + window_ref[by + 7 : by + 8, lanes] * moved[8:]
    return total


def fold_into(u_ref, v_ref, row, group, width, extended_of, window_ref):
    def one(index, carry):
        first = index // (HALF // width) * group
        start = (index % (HALF // width)) * width
        parts = []
        for base in (0, HALF):
            lanes = pl.ds(pl.multiple_of(start + base, width), width)
            parts.append(
                jnp.concatenate(
                    [filtered(extended_of(first + h, lanes), window_ref, lanes) for h in range(group)],
                    axis=0,
                )
            )
        rows = pl.ds(pl.multiple_of(row + index // (HALF // width) * 16, 16), 16)
        lanes = pl.ds(pl.multiple_of(start, width), width)
        u_ref[rows, lanes] = (parts[0] + parts[1]).astype(jnp.bfloat16)
        v_ref[rows, lanes] = (parts[0] - parts[1]).astype(jnp.bfloat16)
        return carry

    lax.fori_loop(0, INS // group * (HALF // width), one, 0)


def own_kernel(core_ref, own_ref, window_ref, u_ref, v_ref):
    second = core_ref[0] == 1

    def extended_of(i, lanes):
        own = own_ref[i, :, lanes].astype(jnp.float32)
        zero = jnp.zeros_like(own)
        return jnp.concatenate([jnp.where(second, own, zero), jnp.where(second, zero, own)], axis=0)

    fold_into(u_ref, v_ref, 0, 1, 512, extended_of, window_ref)


def channel_kernel(
    core_ref, own_ref, other_ref, window_ref, table_any, list_ref, ua_ref, va_ref, out_ref, u_ref, v_ref, table_ref, rows_ref, sems
):
    step = pl.program_id(0)

    @pl.when(step == 0)
    def _():
        for q in range(N_FREQ):
            pltpu.make_async_copy(table_any.at[q], table_ref.at[q], sems.at[q]).start()
        second = core_ref[0] == 1

        def extended_of(i, lanes):
            own = own_ref[i, :, lanes].astype(jnp.float32)
            other = other_ref[i, :, lanes].astype(jnp.float32)
            return jnp.concatenate(
                [
                    jnp.where(second, other[8:], own[:8]),
                    jnp.where(second, own[:8], own[8:]),
                    jnp.where(second, own[8:], other[:8]),
                ],
                axis=0,
            )

        u_ref[:128, :] = ua_ref[...]
        v_ref[:128, :] = va_ref[...]
        u_ref[192:, :] = jnp.zeros((64, HALF), jnp.bfloat16)
        v_ref[192:, :] = jnp.zeros((64, HALF), jnp.bfloat16)
        fold_into(u_ref, v_ref, 128, 2, 512, extended_of, window_ref)

    pltpu.make_async_copy(table_any.at[step], table_ref.at[step], sems.at[step]).wait()
    low = lax.broadcasted_iota(jnp.int32, (1, 128), 1) < 64
    halves = []
    for parity, folded in enumerate((u_ref, v_ref)):
        y = nt_dot(table_ref[step, parity], folded[...])
        re, im = y[:128, :128], y[128:, :128]
        rest = y[:128, 128:] + pltpu.roll(y[128:, 128:], 64, 1)
        first = jnp.where(low, re, pltpu.roll(im, 64, 1))
        last = jnp.where(low, pltpu.roll(re, 64, 1), im)
        halves.append(jnp.concatenate([first, rest, last], axis=1))
    spectra = jnp.concatenate(halves, axis=0).astype(jnp.bfloat16)
    channels = list_ref[0]
    place = (channels & 1) * 128 + ((channels & 255) >> 1)
    picks = (lax.broadcasted_iota(jnp.int32, (QUARTER, QUARTER), 0) == place).astype(jnp.float32)
    picked = jnp.dot(picks.T.astype(jnp.bfloat16), spectra, preferred_element_type=jnp.float32)
    for tile in range(3):
        for slot in range(2):
            rows_ref[pl.ds(tile * 2 + slot, N_BLK, stride=6), :] = picked[
                slot * N_BLK : (slot + 1) * N_BLK, tile * 128 : (tile + 1) * 128
            ]
    out_ref[...] = rows_ref[...].astype(jnp.bfloat16)


def own_part(core, own, window):
    return pl.pallas_call(
        own_kernel,
        in_specs=[
            pl.BlockSpec(memory_space=pltpu.SMEM),
            pl.BlockSpec(memory_space=pltpu.VMEM),
            pl.BlockSpec(memory_space=pltpu.VMEM),
        ],
        out_specs=[pl.BlockSpec(memory_space=pltpu.VMEM)] * 2,
        out_shape=[jax.ShapeDtypeStruct((128, HALF), jnp.bfloat16)] * 2,
        compiler_params=pltpu.CompilerParams(vmem_limit_bytes=57 << 20),
        cost_estimate=pl.CostEstimate(flops=10_000_000, bytes_accessed=2_000_000, transcendentals=0),
        name="own",
    )(core, own, window)


def channel_messages(core, own, other, lists):
    window = jnp.asarray(window_taps())
    table = jnp.asarray(fourier_halves())
    ua, va = own_part(core, own, window)
    half = pl.BlockSpec((128, HALF), lambda q: (0, 0))
    return pl.pallas_call(
        channel_kernel,
        grid=(N_FREQ,),
        in_specs=[
            pl.BlockSpec(memory_space=pltpu.SMEM),
            pl.BlockSpec((INS, 16, FRAME), lambda q: (0, 0, 0)),
            pl.BlockSpec((INS, 16, FRAME), lambda q: (0, 0, 0)),
            pl.BlockSpec((TAPS, FRAME), lambda q: (0, 0)),
            pl.BlockSpec(memory_space=pltpu.HBM),
            pl.BlockSpec((1, 1, QUARTER), lambda q: (q, 0, 0)),
            half,
            half,
        ],
        out_specs=pl.BlockSpec((N_BLK * 6, 128), lambda q: (q % 2 * 2 + q // 2, 0)),
        out_shape=jax.ShapeDtypeStruct((N_FREQ * N_BLK * 6, 128), jnp.bfloat16),
        scratch_shapes=[
            pltpu.VMEM((256, HALF), jnp.bfloat16),
            pltpu.VMEM((256, HALF), jnp.bfloat16),
            pltpu.VMEM(table.shape, jnp.bfloat16),
            pltpu.VMEM((N_BLK * 6, 128), jnp.float32),
            pltpu.SemaphoreType.DMA((N_FREQ,)),
        ],
        compiler_params=pltpu.CompilerParams(vmem_limit_bytes=57 << 20),
        name="channels",
    )(core, own, other, window, table, lists, ua, va)


def correlate_kernel(count_ref, got_ref, merge_ref, out_ref, rows_ref, right_all, even_all, odd_all, left_ref, right_ref):
    slot = pl.program_id(0)

    @pl.when(slot == 0)
    def _():
        sign = jnp.where(lax.broadcasted_iota(jnp.int32, (1, 128), 1) < 64, 1.0, -1.0)
        rows_ref[...] = got_ref[...].astype(jnp.float32)
        sources = {}
        for f in range(N_FREQ):
            for tile in range(3):
                start = (f % 2 * 2 + f // 2) * N_BLK * 6 + tile * 2
                sources[f, tile] = jnp.concatenate(
                    [rows_ref[pl.ds(start + j, N_BLK, stride=6), :] for j in range(2)], axis=0
                ).astype(jnp.bfloat16)
        base = 0
        for pair, tiles in enumerate(GROUPS):
            depth = N_FREQ * len(tiles) * 128
            parts = [sources[f, tile] for f in range(N_FREQ) for tile in tiles]
            both = jnp.dot(
                jnp.concatenate(parts, axis=1),
                merge_ref[base : base + depth, :],
                preferred_element_type=jnp.float32,
            )
            base += depth
            for h in range(2):
                plain = both[:, h * 128 : (h + 1) * 128]
                turned = pltpu.roll(plain, 64, 1) * sign
                right_all[pl.ds(2 * pair + h, 256, stride=8), :] = plain
                left_all = (even_all, odd_all)[h]
                left_all[pl.ds(2 * pair, 256, stride=8), :] = plain
                left_all[pl.ds(2 * pair + 1, 256, stride=8), :] = turned

    live = slot < count_ref[0, 0]

    @pl.when(live)
    def _():
        def tile_of(ref, tile):
            pieces = []
            for b in range(tile * 8, tile * 8 + 8):
                place = b % 4 * 32 + b // 4 % 4 * 8 + b // 16
                pieces.append(ref[pl.ds(pl.multiple_of(slot * 1024 + place * 8, 8), 8), :])
            return jnp.concatenate(pieces, axis=0).astype(jnp.bfloat16)

        for tile in range(TILES):
            rows = slice(tile * 64, tile * 64 + 64)
            left_ref[rows, :128] = tile_of(even_all, tile)
            left_ref[rows, 128:] = tile_of(odd_all, tile)
            right_ref[rows, :] = tile_of(right_all, tile)
        zero = jnp.zeros((64, 128), jnp.bfloat16)
        for m in range(TILES // 2):
            rhs = []
            for q in (2 * m, 2 * m + 1):
                column = right_ref[q * 64 : (q + 1) * 64, :]
                rhs.append(jnp.concatenate([column, zero], axis=1))
                rhs.append(jnp.concatenate([zero, column], axis=1))
            products = nt_dot(left_ref[: (2 * m + 2) * 64, :], jnp.concatenate(rhs, axis=0))
            for h in range(2):
                q = 2 * m + h
                for p in range(q + 1):
                    t = TILES * p - p * (p - 1) // 2 + q - p
                    piece = products[p * 64 : (p + 1) * 64, h * 128 : (h + 1) * 128]
                    out_ref[0, t] = (piece * (1.0 / 64.0)).astype(jnp.bfloat16)

    @pl.when(jnp.logical_not(live))
    def _():
        out_ref[...] = jnp.zeros(out_ref.shape, out_ref.dtype)


def visibility_tiles(counts, got):
    merge = jnp.asarray(merge_matrices())
    return pl.pallas_call(
        correlate_kernel,
        grid=(2,),
        in_specs=[
            pl.BlockSpec(memory_space=pltpu.SMEM),
            pl.BlockSpec((N_FREQ * N_BLK * 6, 128), lambda j: (0, 0)),
            pl.BlockSpec(merge.shape, lambda j: (0, 0)),
        ],
        out_specs=pl.BlockSpec((1, PAIRS, 64, 128), lambda j: (j, 0, 0, 0)),
        out_shape=jax.ShapeDtypeStruct((2, PAIRS, 64, 128), jnp.bfloat16),
        scratch_shapes=[
            pltpu.VMEM((N_FREQ * N_BLK * 6, 128), jnp.float32),
            pltpu.VMEM((2048, 128), jnp.float32),
            pltpu.VMEM((2048, 128), jnp.float32),
            pltpu.VMEM((2048, 128), jnp.float32),
            pltpu.VMEM((1024, 256), jnp.bfloat16),
            pltpu.VMEM((1024, 128), jnp.bfloat16),
        ],
        compiler_params=pltpu.CompilerParams(vmem_limit_bytes=40 << 20),
        name="correlate",
    )(counts, got, merge)


def shards(samples, channel_lists, channel_counts):
    core = lax.axis_index("core").astype(jnp.int32).reshape(1)
    other = lax.ppermute(samples, "core", [(0, 1), (1, 0)])
    lists = channel_lists.reshape(N_FREQ, 8, 4, 4, 2).transpose(0, 4, 3, 2, 1).reshape(N_FREQ, 1, QUARTER)
    messages = channel_messages(core, samples, other, lists)
    got = lax.all_to_all(
        messages.reshape(N_FREQ * N_BLK, 3, 2, 128), ("core", "z_hi", "x", "y", "z_lo"), 0, 0, tiled=True
    ).reshape(N_FREQ * N_BLK * 6, 128)
    tiles = visibility_tiles(channel_counts, got)
    tiles = tiles.reshape(2, PAIRS, 32, 2, 128).transpose(0, 1, 3, 2, 4)
    return tiles.reshape(1, 1, 2, PAIRS, 2, 4096)


def solution(mesh):
    fine = Mesh(mesh.devices.reshape(8, 4, 4, 2, 2), ("z_lo", "y", "x", "z_hi", "core"))
    blk, freq = ("z_lo", "y", "x"), ("z_hi", "core")
    in_specs = (P(blk, freq, None), P(), P(freq, blk))
    out_specs = P(freq, blk, None, None, None, None)
    return jax.shard_map(shards, mesh=fine, in_specs=in_specs, out_specs=out_specs, check_vma=False)
```

time: 94.3 us -> 91.1 us (0.966)
  local copies, waits for them, and re-layouts: 8.48 us -> 2.66 us
  Pallas kernels: 11 us -> 16.2 us
  starting transfers between devices: 28.4 us -> 26.3 us
    pallas_call x0 -> x1, Pallas kernels: none -> 4.91 us  [own_part(): pl.pallas_call(own_kernel, in_specs=[pl.BlockSpec(memory_space=pltpu.SMEM...]
    unnamed x9 -> x4, local copies, waits for them, and re-layouts: 4.97 us -> 0.79 us
    all_to_all x1, starting transfers between devices: 19.6 us -> 17.5 us  [shards(): lax.all_to_all(messages.reshape(N_FREQ * N_BLK, 3, 2, 128), ('core', 'z_h...]
    reshape x3 -> x2, local copies, waits for them, and re-layouts: 3.52 us -> 1.61 us  [shards(): channel_lists.reshape(N_FREQ, 8, 4, 4, 2).transpose(0, 4, 3, 2, 1)]
  transfers between devices with their start and end apart: 2 -> 2, of which waited for: 2 -> 1; matrix products, arithmetic and copies ran while one was open for 1% -> 2% of each run, Pallas kernels for 0% -> 5%
where the time goes in v1:
time: 91.1 us; the launch traced here: 90.8 us
  waiting for transfers between devices  45 us (49%)
  starting transfers between devices  26.3 us (29%)
  Pallas kernels  16.2 us (18%)
  local copies, waits for them, and re-layouts  2.66 us (3%)
    all_to_all x1, waiting for transfers between devices, shards(): lax.all_to_all(messages.reshape(N_FREQ * N_BLK, 3, 2, 128), ('core', 'z_h...  45 us
    all_to_all x1, starting transfers between devices, shards(): lax.all_to_all(messages.reshape(N_FREQ * N_BLK, 3, 2, 128), ('core', 'z_h...  17.5 us
    ppermute x1, starting transfers between devices, shards(): other = lax.ppermute(samples, 'core', [(0, 1), (1, 0)])  8.78 us
    pallas_call x1, Pallas kernels, channel_messages(): pl.pallas_call(channel_kernel, grid=(N_FREQ,), in_specs=[pl.BlockSpec(mem...  7.25 us
    pallas_call x1, Pallas kernels, own_part(): pl.pallas_call(own_kernel, in_specs=[pl.BlockSpec(memory_space=pltpu.SMEM...  4.91 us
    pallas_call x1, Pallas kernels, visibility_tiles(): pl.pallas_call(correlate_kernel, grid=(2,), in_specs=[pl.BlockSpec(memory...  4.03 us
  transfers between devices with their start and end apart: 2, of which 1 were waited for; matrix products, arithmetic and copies ran while one was open for 2% of the time, Pallas kernels for 5%

profile of v1, /device:TPU:1, one launch (start us, length us, event | category | flops | bytes accessed | tf_op | source)
XLA Modules:
  0.0 90.8 jit_solution(14377045133125966601)
XLA Ops:
  0.0 8.8 %collective-permute-start = (bf16[8,16,2048]{2,1,0:T(8,128)(2,1)}, bf16[8,16,2048]{2,1,0:T(8,128)(2,1)S(1)}, u32[]{:S(2)}, u32[]{:S(2)}) collective-permute-start(bf16[8,16,2048]{2,1,0:T(8,128)(2,1)} %own_ref.3), channel_id=1, source_target_pairs={{0,1},{1,0},{2,3},{3,2},{4,5},{5,4},{6,7},{7,6},{8,9},{9,8},{10,11... | collective-permute-start | bytes 1572872 | tf_op jit(solution)/shard_map/ppermute | solution.py:309
  8.8 0.9 reshape.22
  9.7 0.3 copy.9
  9.9 0.7 reshape.23.list_ref
  10.7 4.9 %own.1 = (bf16[128,1024]{1,0:T(8,128)(2,1)}, bf16[128,1024]{1,0:T(8,128)(2,1)}) custom-call(s32[1]{0:T(128)} %bitcast.core_ref, bf16[8,16,2048]{2,1,0:T(8,128)(2,1)} %own_ref.3, f32[16,2048]{1,0:T(8,128)} %constant.10.clone.window_ref), custom_call_target="tpu_custom_call" | custom-call | flops 10000000 | bytes 2000000 | tf_op jit(solution)/shard_map/own/pallas_call | solution.py:167
  15.6 0.0 copy-start
  15.6 0.0 collective-permute-done.other_ref
  15.6 0.0 copy-start.1
  15.6 0.8 copy-done.1
  16.4 7.3 %channels.1 = bf16[3072,128]{1,0:T(8,128)(2,1)} custom-call(s32[1]{0:T(128)} %bitcast.core_ref, bf16[8,16,2048]{2,1,0:T(8,128)(2,1)} %own_ref.3, bf16[8,16,2048]{2,1,0:T(8,128)(2,1)} %copy-done.1, f32[16,2048]{1,0:T(8,128)} %constant.10.clone.window_ref, bf16[4,2,256,1024]{3,2,1,0:T(8,128)(2,1)} %constant.11.clone.table_any, s32[4,1,256]{2,1,0:T(1,128)} %reshape.23.list_ref, ...), custom_call_target="tpu_custom_call" | custom-call | tf_op jit(solution)/shard_map/channels/pallas_call | solution.py:187
  23.6 17.5 %all-to-all-start = ((bf16[512,3,2,128]{3,2,1,0:T(2,128)(2,1)}), bf16[512,3,2,128]{3,2,1,0:T(2,128)(2,1)S(1)}, u32[]{:S(2)}, u32[]{:S(2)}) async-start(bf16[512,3,2,128]{3,2,1,0:T(2,128)(2,1)} %bitcast.12), calls=%async_computation | async-start | bytes 1572864 | tf_op jit(solution)/shard_map/all_to_all | solution.py:312
  41.8 45.0 %all-to-all-done = bf16[512,3,2,128]{3,2,1,0:T(2,128)(2,1)S(1)} async-done(((bf16[512,3,2,128]{3,2,1,0:T(2,128)(2,1)}), bf16[512,3,2,128]{3,2,1,0:T(2,128)(2,1)S(1)}, u32[]{:S(2)}, u32[]{:S(2)}) %all-to-all-start) | async-done | bytes 786464 | tf_op jit(solution)/shard_map/all_to_all | solution.py:312
  86.8 0.0 copy-done
  86.8 4.0 %correlate.1 = bf16[2,136,64,128]{3,2,1,0:T(8,128)(2,1)} custom-call(s32[1,1]{1,0:T(1,128)S(6)} %copy.11.count_ref, bf16[3072,128]{1,0:T(8,128)(2,1)S(1)} %bitcast.11, bf16[4096,256]{1,0:T(8,128)(2,1)S(1)} %copy-done), custom_call_target="tpu_custom_call" | custom-call | tf_op jit(solution)/shard_map/correlate/pallas_call | solution.py:284
Async XLA Ops:
  0.0 15.6 %collective-permute-start = (bf16[8,16,2048]{2,1,0:T(8,128)(2,1)}, bf16[8,16,2048]{2,1,0:T(8,128)(2,1)S(1)}, u32[]{:S(2)}, u32[]{:S(2)}) collective-permute-start(bf16[8,16,2048]{2,1,0:T(8,128)(2,1)} %own_ref.3), channel_id=1, source_target_pairs={{0,1},{1,0},{2,3},{3,2},{4,5},{5,4},{6,7},{7,6},{8,9},{9,8},{10,11... | collective-permute-start | bytes 1572872 | tf_op jit(solution)/shard_map/ppermute | solution.py:309
  15.6 71.2 %copy-start = (bf16[4096,256]{1,0:T(8,128)(2,1)S(1)}, bf16[4096,256]{1,0:T(8,128)(2,1)}, u32[]{:S(2)}) copy-start(bf16[4096,256]{1,0:T(8,128)(2,1)} %constant.12.clone.merge_ref) | copy-start | bytes 6291460
  15.6 0.8 copy-start.1
  23.6 63.2 %all-to-all-start = ((bf16[512,3,2,128]{3,2,1,0:T(2,128)(2,1)}), bf16[512,3,2,128]{3,2,1,0:T(2,128)(2,1)S(1)}, u32[]{:S(2)}, u32[]{:S(2)}) async-start(bf16[512,3,2,128]{3,2,1,0:T(2,128)(2,1)} %bitcast.12), calls=%async_computation | async-start | bytes 1572864 | tf_op jit(solution)/shard_map/all_to_all | solution.py:312

commit v2 on v1

--- a/solution.py
+++ b/solution.py
@@ -78,29 +78,40 @@
     return total
 
 
-def fold_into(u_ref, v_ref, row, group, width, extended_of, window_ref):
+def fold_into(u_ref, v_ref, row, inputs, group, width, extended_of, window_ref):
     def one(index, carry):
-        first = index // (HALF // width) * group
+        step = index // (HALF // width)
         start = (index % (HALF // width)) * width
         parts = []
         for base in (0, HALF):
             lanes = pl.ds(pl.multiple_of(start + base, width), width)
             parts.append(
                 jnp.concatenate(
-                    [filtered(extended_of(first + h, lanes), window_ref, lanes) for h in range(group)],
+                    [
+                        filtered(extended_of(inputs[0] + step * group + h, lanes), window_ref, lanes)
+                        for h in range(group)
+                    ],
                     axis=0,
                 )
             )
-        rows = pl.ds(pl.multiple_of(row + index // (HALF // width) * 16, 16), 16)
+        rows = pl.ds(pl.multiple_of(row + step * 16, 16), 16)
         lanes = pl.ds(pl.multiple_of(start, width), width)
         u_ref[rows, lanes] = (parts[0] + parts[1]).astype(jnp.bfloat16)
         v_ref[rows, lanes] = (parts[0] - parts[1]).astype(jnp.bfloat16)
         return carry
 
-    lax.fori_loop(0, INS // group * (HALF // width), one, 0)
-
-
-def own_kernel(core_ref, own_ref, window_ref, u_ref, v_ref):
+    lax.fori_loop(0, len(inputs) // group * (HALF // width), one, 0)
+
+
+def own_kernel(core_ref, own_hbm, window_hbm, table_hbm, u_ref, v_ref, own_ref, window_ref, table_ref, sems):
+    window_copy = pltpu.make_async_copy(window_hbm, window_ref, sems.at[0])
+    table_copy = pltpu.make_async_copy(table_hbm, table_ref, sems.at[1])
+    own_copies = [
+        pltpu.make_async_copy(own_hbm.at[c : c + 2], own_ref.at[c : c + 2], sems.at[2 + c // 2])
+        for c in range(0, INS, 2)
+    ]
+    for copy in [window_copy, *own_copies, table_copy]:
+        copy.start()
     second = core_ref[0] == 1
 
     def extended_of(i, lanes):
@@ -108,105 +119,93 @@
         zero = jnp.zeros_like(own)
         return jnp.concatenate([jnp.where(second, own, zero), jnp.where(second, zero, own)], axis=0)
 
-    fold_into(u_ref, v_ref, 0, 1, 512, extended_of, window_ref)
+    window_copy.wait()
+    for c, copy in enumerate(own_copies):
+        copy.wait()
+        fold_into(u_ref, v_ref, c * 32, range(2 * c, 2 * c + 2), 1, 512, extended_of, window_ref)
+    table_copy.wait()
 
 
 def channel_kernel(
-    core_ref, own_ref, other_ref, window_ref, table_any, list_ref, ua_ref, va_ref, out_ref, u_ref, v_ref, table_ref, rows_ref, sems
+    core_ref, own_ref, other_ref, window_ref, table_ref, list_ref, ua_ref, va_ref, out_ref, u_ref, v_ref, rows_ref
 ):
-    step = pl.program_id(0)
-
-    @pl.when(step == 0)
-    def _():
-        for q in range(N_FREQ):
-            pltpu.make_async_copy(table_any.at[q], table_ref.at[q], sems.at[q]).start()
-        second = core_ref[0] == 1
-
-        def extended_of(i, lanes):
-            own = own_ref[i, :, lanes].astype(jnp.float32)
-            other = other_ref[i, :, lanes].astype(jnp.float32)
-            return jnp.concatenate(
-                [
-                    jnp.where(second, other[8:], own[:8]),
-                    jnp.where(second, own[:8], own[8:]),
-                    jnp.where(second, own[8:], other[:8]),
-                ],
-                axis=0,
-            )
-
-        u_ref[:128, :] = ua_ref[...]
-        v_ref[:128, :] = va_ref[...]
-        u_ref[192:, :] = jnp.zeros((64, HALF), jnp.bfloat16)
-        v_ref[192:, :] = jnp.zeros((64, HALF), jnp.bfloat16)
-        fold_into(u_ref, v_ref, 128, 2, 512, extended_of, window_ref)
-
-    pltpu.make_async_copy(table_any.at[step], table_ref.at[step], sems.at[step]).wait()
+    second = core_ref[0] == 1
+
+    def extended_of(i, lanes):
+        own = own_ref[i, :, lanes].astype(jnp.float32)
+        other = other_ref[i, :, lanes].astype(jnp.float32)
+        return jnp.concatenate(
+            [
+                jnp.where(second, other[8:], own[:8]),
+                jnp.where(second, own[:8], own[8:]),
+                jnp.where(second, own[8:], other[:8]),
+            ],
+            axis=0,
+        )
+
+    u_ref[:128, :] = ua_ref[...]
+    v_ref[:128, :] = va_ref[...]
+    u_ref[192:, :] = jnp.zeros((64, HALF), jnp.bfloat16)
+    v_ref[192:, :] = jnp.zeros((64, HALF), jnp.bfloat16)
+    fold_into(u_ref, v_ref, 128, range(INS), 2, 512, extended_of, window_ref)
+
     low = lax.broadcasted_iota(jnp.int32, (1, 128), 1) < 64
-    halves = []
-    for parity, folded in enumerate((u_ref, v_ref)):
-        y = nt_dot(table_ref[step, parity], folded[...])
-        re, im = y[:128, :128], y[128:, :128]
-        rest = y[:128, 128:] + pltpu.roll(y[128:, 128:], 64, 1)
-        first = jnp.where(low, re, pltpu.roll(im, 64, 1))
-        last = jnp.where(low, pltpu.roll(re, 64, 1), im)
-        halves.append(jnp.concatenate([first, rest, last], axis=1))
-    spectra = jnp.concatenate(halves, axis=0).astype(jnp.bfloat16)
-    channels = list_ref[0]
-    place = (channels & 1) * 128 + ((channels & 255) >> 1)
-    picks = (lax.broadcasted_iota(jnp.int32, (QUARTER, QUARTER), 0) == place).astype(jnp.float32)
-    picked = jnp.dot(picks.T.astype(jnp.bfloat16), spectra, preferred_element_type=jnp.float32)
-    for tile in range(3):
-        for slot in range(2):
-            rows_ref[pl.ds(tile * 2 + slot, N_BLK, stride=6), :] = picked[
-                slot * N_BLK : (slot + 1) * N_BLK, tile * 128 : (tile + 1) * 128
-            ]
+    for q in range(N_FREQ):
+        halves = []
+        for parity, folded in enumerate((u_ref, v_ref)):
+            y = nt_dot(table_ref[q, parity], folded[...])
+            re, im = y[:128, :128], y[128:, :128]
+            rest = y[:128, 128:] + pltpu.roll(y[128:, 128:], 64, 1)
+            first = jnp.where(low, re, pltpu.roll(im, 64, 1))
+            last = jnp.where(low, pltpu.roll(re, 64, 1), im)
+            halves.append(jnp.concatenate([first, rest, last], axis=1))
+        spectra = jnp.concatenate(halves, axis=0).astype(jnp.bfloat16)
+        channels = list_ref[q]
+        place = (channels & 1) * 128 + ((channels & 255) >> 1)
+        place = jnp.concatenate([place[:1], place[1:]], axis=1)
+        picks = (lax.broadcasted_iota(jnp.int32, (QUARTER, QUARTER), 0) == place).astype(jnp.float32)
+        picked = jnp.dot(picks.T.astype(jnp.bfloat16), spectra, preferred_element_type=jnp.float32)
+        for tile in range(3):
+            for slot in range(2):
+                rows_ref[pl.ds(q * 6 + tile * 2 + slot, N_BLK, stride=N_FREQ * 6), :] = picked[
+                    slot * N_BLK : (slot + 1) * N_BLK, tile * 128 : (tile + 1) * 128
+                ]
     out_ref[...] = rows_ref[...].astype(jnp.bfloat16)
 
 
-def own_part(core, own, window):
+def own_part(core, own, window, table):
+    hbm = pl.BlockSpec(memory_space=pltpu.HBM)
+    vmem = pl.BlockSpec(memory_space=pltpu.VMEM)
+    pinned = [pltpu.with_memory_space_constraint(x, pltpu.HBM) for x in (own, window, table)]
+    half = pltpu.VMEM((128, HALF), jnp.bfloat16)
     return pl.pallas_call(
         own_kernel,
-        in_specs=[
-            pl.BlockSpec(memory_space=pltpu.SMEM),
-            pl.BlockSpec(memory_space=pltpu.VMEM),
-            pl.BlockSpec(memory_space=pltpu.VMEM),
-        ],
-        out_specs=[pl.BlockSpec(memory_space=pltpu.VMEM)] * 2,
-        out_shape=[jax.ShapeDtypeStruct((128, HALF), jnp.bfloat16)] * 2,
-        compiler_params=pltpu.CompilerParams(vmem_limit_bytes=57 << 20),
+        in_specs=[pl.BlockSpec(memory_space=pltpu.SMEM), hbm, hbm, hbm],
+        out_specs=[vmem] * 5,
+        out_shape=[half, half, *(pltpu.VMEM(x.shape, x.dtype) for x in (own, window, table))],
+        scratch_shapes=[pltpu.SemaphoreType.DMA((6,))],
+        compiler_params=pltpu.CompilerParams(vmem_limit_bytes=24 << 20),
         cost_estimate=pl.CostEstimate(flops=10_000_000, bytes_accessed=2_000_000, transcendentals=0),
         name="own",
-    )(core, own, window)
+    )(core, *pinned)
 
 
 def channel_messages(core, own, other, lists):
     window = jnp.asarray(window_taps())
     table = jnp.asarray(fourier_halves())
-    ua, va = own_part(core, own, window)
-    half = pl.BlockSpec((128, HALF), lambda q: (0, 0))
+    ua, va, own, window, table = own_part(core, own, window, table)
+    vmem = pl.BlockSpec(memory_space=pltpu.VMEM)
     return pl.pallas_call(
         channel_kernel,
-        grid=(N_FREQ,),
-        in_specs=[
-            pl.BlockSpec(memory_space=pltpu.SMEM),
-            pl.BlockSpec((INS, 16, FRAME), lambda q: (0, 0, 0)),
-            pl.BlockSpec((INS, 16, FRAME), lambda q: (0, 0, 0)),
-            pl.BlockSpec((TAPS, FRAME), lambda q: (0, 0)),
-            pl.BlockSpec(memory_space=pltpu.HBM),
-            pl.BlockSpec((1, 1, QUARTER), lambda q: (q, 0, 0)),
-            half,
-            half,
-        ],
-        out_specs=pl.BlockSpec((N_BLK * 6, 128), lambda q: (q % 2 * 2 + q // 2, 0)),
+        in_specs=[pl.BlockSpec(memory_space=pltpu.SMEM)] + [vmem] * 7,
+        out_specs=vmem,
         out_shape=jax.ShapeDtypeStruct((N_FREQ * N_BLK * 6, 128), jnp.bfloat16),
         scratch_shapes=[
             pltpu.VMEM((256, HALF), jnp.bfloat16),
             pltpu.VMEM((256, HALF), jnp.bfloat16),
-            pltpu.VMEM(table.shape, jnp.bfloat16),
-            pltpu.VMEM((N_BLK * 6, 128), jnp.float32),
-            pltpu.SemaphoreType.DMA((N_FREQ,)),
+            pltpu.VMEM((N_FREQ * N_BLK * 6, 128), jnp.float32),
         ],
-        compiler_params=pltpu.CompilerParams(vmem_limit_bytes=57 << 20),
+        compiler_params=pltpu.CompilerParams(vmem_limit_bytes=32 << 20),
         name="channels",
     )(core, own, other, window, table, lists, ua, va)
 
@@ -221,9 +220,9 @@
         sources = {}
         for f in range(N_FREQ):
             for tile in range(3):
-                start = (f % 2 * 2 + f // 2) * N_BLK * 6 + tile * 2
+                start = f * 6 + tile * 2
                 sources[f, tile] = jnp.concatenate(
-                    [rows_ref[pl.ds(start + j, N_BLK, stride=6), :] for j in range(2)], axis=0
+                    [rows_ref[pl.ds(start + j, N_BLK, stride=N_FREQ * 6), :] for j in range(2)], axis=0
                 ).astype(jnp.bfloat16)
         base = 0
         for pair, tiles in enumerate(GROUPS):
@@ -248,11 +247,7 @@
     @pl.when(live)
     def _():
         def tile_of(ref, tile):
-            pieces = []
-            for b in range(tile * 8, tile * 8 + 8):
-                place = b % 4 * 32 + b // 4 % 4 * 8 + b // 16
-                pieces.append(ref[pl.ds(pl.multiple_of(slot * 1024 + place * 8, 8), 8), :])
-            return jnp.concatenate(pieces, axis=0).astype(jnp.bfloat16)
+            return ref[pl.ds(pl.multiple_of(slot * 1024 + tile * 64, 64), 64), :].astype(jnp.bfloat16)
 
         for tile in range(TILES):
             rows = slice(tile * 64, tile * 64 + 64)
@@ -307,10 +302,10 @@
 def shards(samples, channel_lists, channel_counts):
     core = lax.axis_index("core").astype(jnp.int32).reshape(1)
     other = lax.ppermute(samples, "core", [(0, 1), (1, 0)])
-    lists = channel_lists.reshape(N_FREQ, 8, 4, 4, 2).transpose(0, 4, 3, 2, 1).reshape(N_FREQ, 1, QUARTER)
+    lists = channel_lists.transpose(0, 2, 1)
     messages = channel_messages(core, samples, other, lists)
     got = lax.all_to_all(
-        messages.reshape(N_FREQ * N_BLK, 3, 2, 128), ("core", "z_hi", "x", "y", "z_lo"), 0, 0, tiled=True
+        messages.reshape(N_FREQ * N_BLK, 3, 2, 128), ("z_lo", "y", "x", "z_hi", "core"), 0, 0, tiled=True
     ).reshape(N_FREQ * N_BLK * 6, 128)
     tiles = visibility_tiles(channel_counts, got)
     tiles = tiles.reshape(2, PAIRS, 32, 2, 128).transpose(0, 1, 3, 2, 4)

time: 91.1 us -> 87.2 us (0.957)
  Pallas kernels: 16.2 us -> 13.2 us
  local copies, waits for them, and re-layouts: 2.66 us -> 0.01 us
  waiting for transfers between devices: 45 us -> 46.7 us
    pallas_call x1, Pallas kernels: 7.25 us -> 5.48 us  [channel_messages(): pl.pallas_call(channel_kernel, in_specs=[pl.BlockSpec(memory_space=pltpu....]
    all_to_all x1, waiting for transfers between devices: 45 us -> 46.7 us  [shards(): lax.all_to_all(messages.reshape(N_FREQ * N_BLK, 3, 2, 128), ('z_lo', 'y',...]
    reshape x2 -> x0, local copies, waits for them, and re-layouts: 1.61 us -> none  [shards(): channel_lists.reshape(N_FREQ, 8, 4, 4, 2).transpose(0, 4, 3, 2, 1)]
  transfers between devices with their start and end apart: 2 -> 2, of which waited for: 1 -> 1; matrix products, arithmetic and copies ran while one was open for 2% -> 0% of each run, Pallas kernels for 5% -> 5%
where the time goes in v2:
time: 87.2 us; the launch traced here: 87 us
  waiting for transfers between devices  46.7 us (54%)
  starting transfers between devices  26.4 us (30%)
  Pallas kernels  13.2 us (15%)
    all_to_all x1, waiting for transfers between devices, shards(): lax.all_to_all(messages.reshape(N_FREQ * N_BLK, 3, 2, 128), ('z_lo', 'y',...  46.7 us
    all_to_all x1, starting transfers between devices, shards(): lax.all_to_all(messages.reshape(N_FREQ * N_BLK, 3, 2, 128), ('z_lo', 'y',...  17.5 us
    ppermute x1, starting transfers between devices, shards(): other = lax.ppermute(samples, 'core', [(0, 1), (1, 0)])  8.91 us
    pallas_call x1, Pallas kernels, channel_messages(): pl.pallas_call(channel_kernel, in_specs=[pl.BlockSpec(memory_space=pltpu....  5.48 us
    pallas_call x1, Pallas kernels, own_part(): pl.pallas_call(own_kernel, in_specs=[pl.BlockSpec(memory_space=pltpu.SMEM...  4.18 us
    pallas_call x1, Pallas kernels, visibility_tiles(): pl.pallas_call(correlate_kernel, grid=(2,), in_specs=[pl.BlockSpec(memory...  3.52 us
  transfers between devices with their start and end apart: 2, of which 1 were waited for; matrix products, arithmetic and copies ran while one was open for 0% of the time, Pallas kernels for 5%

profile of v2, /device:TPU:1, one launch (start us, length us, event | category | flops | bytes accessed | tf_op | source)
XLA Modules:
  0.0 87.0 jit_solution(2105597770531420692)
XLA Ops:
  0.0 0.0 copy-start.1
  0.0 8.9 %collective-permute-start = (bf16[8,16,2048]{2,1,0:T(8,128)(2,1)}, bf16[8,16,2048]{2,1,0:T(8,128)(2,1)S(1)}, u32[]{:S(2)}, u32[]{:S(2)}) collective-permute-start(bf16[8,16,2048]{2,1,0:T(8,128)(2,1)} %own_hbm.1), channel_id=1, source_target_pairs={{0,1},{1,0},{2,3},{3,2},{4,5},{5,4},{6,7},{7,6},{8,9},{9,8},{10,11... | collective-permute-start | bytes 1572872 | tf_op jit(solution)/shard_map/ppermute | solution.py:304
  8.9 4.2 %own.1 = (bf16[128,1024]{1,0:T(8,128)(2,1)S(1)}, bf16[128,1024]{1,0:T(8,128)(2,1)S(1)}, bf16[8,16,2048]{2,1,0:T(8,128)(2,1)S(1)}, f32[16,2048]{1,0:T(8,128)S(1)}, bf16[4,2,256,1024]{3,2,1,0:T(8,128)(2,1)S(1)}) custom-call(s32[1]{0:T(128)} %bitcast.core_ref, bf16[8,16,2048]{2,1,0:T(8,128)(2,1)} %own_hbm.1, f32[16,2048]{1,0:T(8,128)} %constant.10.clone.window_hbm, ...), custom_call_target="tpu_custom_call" | custom-call | flops 10000000 | bytes 2000000 | tf_op jit(solution)/shard_map/own/pallas_call | solution.py:181
  13.1 0.0 copy-start
  13.1 0.0 collective-permute-done.other_ref
  13.1 0.0 copy-done.1
  13.1 5.5 %channels.1 = bf16[3072,128]{1,0:T(8,128)(2,1)} custom-call(s32[1]{0:T(128)} %bitcast.core_ref, bf16[8,16,2048]{2,1,0:T(8,128)(2,1)S(1)} %get-tuple-element.10.own_ref, bf16[8,16,2048]{2,1,0:T(8,128)(2,1)S(1)} %collective-permute-done.other_ref, f32[16,2048]{1,0:T(8,128)S(1)} %get-tuple-element.11.window_ref, ...), custom_call_target="tpu_custom_call" | custom-call | tf_op jit(solution)/shard_map/channels/pallas_call | solution.py:198
  18.6 17.5 %all-to-all-start = ((bf16[512,3,2,128]{3,2,1,0:T(2,128)(2,1)}), bf16[512,3,2,128]{3,2,1,0:T(2,128)(2,1)S(1)}, u32[]{:S(2)}, u32[]{:S(2)}) async-start(bf16[512,3,2,128]{3,2,1,0:T(2,128)(2,1)} %bitcast.2), calls=%async_computation | async-start | bytes 1572864 | tf_op jit(solution)/shard_map/all_to_all | solution.py:307
  36.8 46.7 %all-to-all-done = bf16[512,3,2,128]{3,2,1,0:T(2,128)(2,1)S(1)} async-done(((bf16[512,3,2,128]{3,2,1,0:T(2,128)(2,1)}), bf16[512,3,2,128]{3,2,1,0:T(2,128)(2,1)S(1)}, u32[]{:S(2)}, u32[]{:S(2)}) %all-to-all-start) | async-done | bytes 786464 | tf_op jit(solution)/shard_map/all_to_all | solution.py:307
  83.5 0.0 copy-done
  83.5 3.5 %correlate.1 = bf16[2,136,64,128]{3,2,1,0:T(8,128)(2,1)} custom-call(s32[1,1]{1,0:T(1,128)S(6)} %copy.8.count_ref, bf16[3072,128]{1,0:T(8,128)(2,1)S(1)} %bitcast.9, bf16[4096,256]{1,0:T(8,128)(2,1)S(1)} %copy-done), custom_call_target="tpu_custom_call" | custom-call | tf_op jit(solution)/shard_map/correlate/pallas_call | solution.py:279
Async XLA Ops:
  0.0 13.1 %copy-start.1 = (s32[4,128,2]{1,2,0:T(2,128)S(1)}, s32[4,128,2]{1,2,0:T(2,128)}, u32[]{:S(2)}) copy-start(s32[4,128,2]{1,2,0:T(2,128)} %param.7) | copy-start | bytes 12292
  0.0 13.1 %collective-permute-start = (bf16[8,16,2048]{2,1,0:T(8,128)(2,1)}, bf16[8,16,2048]{2,1,0:T(8,128)(2,1)S(1)}, u32[]{:S(2)}, u32[]{:S(2)}) collective-permute-start(bf16[8,16,2048]{2,1,0:T(8,128)(2,1)} %own_hbm.1), channel_id=1, source_target_pairs={{0,1},{1,0},{2,3},{3,2},{4,5},{5,4},{6,7},{7,6},{8,9},{9,8},{10,11... | collective-permute-start | bytes 1572872 | tf_op jit(solution)/shard_map/ppermute | solution.py:304
  13.1 70.4 %copy-start = (bf16[4096,256]{1,0:T(8,128)(2,1)S(1)}, bf16[4096,256]{1,0:T(8,128)(2,1)}, u32[]{:S(2)}) copy-start(bf16[4096,256]{1,0:T(8,128)(2,1)} %constant.12.clone.merge_ref) | copy-start | bytes 6291460
  18.6 64.9 %all-to-all-start = ((bf16[512,3,2,128]{3,2,1,0:T(2,128)(2,1)}), bf16[512,3,2,128]{3,2,1,0:T(2,128)(2,1)S(1)}, u32[]{:S(2)}, u32[]{:S(2)}) async-start(bf16[512,3,2,128]{3,2,1,0:T(2,128)(2,1)} %bitcast.2), calls=%async_computation | async-start | bytes 1572864 | tf_op jit(solution)/shard_map/all_to_all | solution.py:307

commit v3 on v2

--- a/solution.py
+++ b/solution.py
@@ -19,7 +19,7 @@
 N_FREQ = 4
 TILES = 16
 PAIRS = 136
-GROUPS = ((0, 1), (0, 1), (1, 2), (1, 2))
+GROUPS = ((0, 1, 2),) * 4
 
 
 def window_taps():
@@ -41,9 +41,10 @@
 
 
 def message_lane(core, i, t, r):
-    if 16 * core <= 2 * t < 32 + 16 * core:
-        return i // 4 * 256 + 64 * r + i % 4 * 16 + t - 8 * core
-    return 128 + 64 * r + i * 8 + t % 8
+    own = t - 8 * core
+    if 0 <= own < 16:
+        return own // 8 * 256 + 64 * r + own % 8 * 8 + i
+    return 128 + 64 * r + t % 8 * 8 + i
 
 
 def merge_matrices():
@@ -68,92 +69,114 @@
     return lax.dot_general(a, b, (((1,), (1,)), ((), ())), preferred_element_type=jnp.float32)
 
 
-def filtered(extended, window_ref, lanes):
-    count = extended.shape[0] - 16
-    total = window_ref[7:8, lanes] * extended[8 : 8 + count] + window_ref[15:16, lanes] * extended[16:]
-    for by in range(1, 8):
-        moved = extended[by : by + count + 8]
-        total = total + window_ref[by - 1 : by, lanes] * moved[:count]
-        total = total + window_ref[by + 7 : by + 8, lanes] * moved[8:]
-    return total
-
-
-def fold_into(u_ref, v_ref, row, inputs, group, width, extended_of, window_ref):
-    def one(index, carry):
-        step = index // (HALF // width)
-        start = (index % (HALF // width)) * width
+def spread(block_ref, first, frames, into_ref):
+    for i in range(INS):
+        for tile in range(FRAME // 128):
+            values = block_ref[i, :, tile * 128 : (tile + 1) * 128].astype(jnp.float32)
+            into_ref[pl.ds(tile * frames * 8 + i, frames, stride=8), :] = values[first : first + frames]
+
+
+def fold_into(u_ref, v_ref, row, outputs, terms_of, frame_of, window_ref):
+    def one(tile, carry):
         parts = []
-        for base in (0, HALF):
-            lanes = pl.ds(pl.multiple_of(start + base, width), width)
-            parts.append(
-                jnp.concatenate(
-                    [
-                        filtered(extended_of(inputs[0] + step * group + h, lanes), window_ref, lanes)
-                        for h in range(group)
-                    ],
-                    axis=0,
-                )
-            )
-        rows = pl.ds(pl.multiple_of(row + step * 16, 16), 16)
-        lanes = pl.ds(pl.multiple_of(start, width), width)
-        u_ref[rows, lanes] = (parts[0] + parts[1]).astype(jnp.bfloat16)
-        v_ref[rows, lanes] = (parts[0] - parts[1]).astype(jnp.bfloat16)
+        for half in (tile, tile + HALF // 128):
+            lanes = pl.ds(pl.multiple_of(half * 128, 128), 128)
+            taps = [jnp.broadcast_to(window_ref[k : k + 1, lanes], (8, 128)) for k in range(TAPS)]
+            frames = {}
+            totals = []
+            for t in range(outputs):
+                total = jnp.zeros((8, 128), jnp.float32)
+                for k, m in terms_of(t):
+                    if m not in frames:
+                        frames[m] = frame_of(m, half)
+                    total = total + taps[k] * frames[m]
+                totals.append(total)
+            parts.append(totals)
+        lanes = pl.ds(pl.multiple_of(tile * 128, 128), 128)
+        for t in range(0, outputs, 2):
+            low = jnp.concatenate(parts[0][t : t + 2], axis=0)
+            high = jnp.concatenate(parts[1][t : t + 2], axis=0)
+            u_ref[row + t * 8 : row + t * 8 + 16, lanes] = (low + high).astype(jnp.bfloat16)
+            v_ref[row + t * 8 : row + t * 8 + 16, lanes] = (low - high).astype(jnp.bfloat16)
         return carry
 
-    lax.fori_loop(0, len(inputs) // group * (HALF // width), one, 0)
-
-
-def own_kernel(core_ref, own_hbm, window_hbm, table_hbm, u_ref, v_ref, own_ref, window_ref, table_ref, sems):
-    window_copy = pltpu.make_async_copy(window_hbm, window_ref, sems.at[0])
-    table_copy = pltpu.make_async_copy(table_hbm, table_ref, sems.at[1])
-    own_copies = [
-        pltpu.make_async_copy(own_hbm.at[c : c + 2], own_ref.at[c : c + 2], sems.at[2 + c // 2])
-        for c in range(0, INS, 2)
+    lax.fori_loop(0, HALF // 128, one, 0)
+
+
+def own_kernel(core_ref, own_hbm, window_hbm, table_hbm, u_ref, v_ref, frames_ref, window_ref, table_ref, own_ref, sems):
+    copies = [
+        pltpu.make_async_copy(own_hbm, own_ref, sems.at[0]),
+        pltpu.make_async_copy(window_hbm, window_ref, sems.at[1]),
+        pltpu.make_async_copy(table_hbm, table_ref, sems.at[2]),
     ]
-    for copy in [window_copy, *own_copies, table_copy]:
+    for copy in copies:
         copy.start()
+    copies[0].wait()
+    spread(own_ref, 0, 16, frames_ref)
+    copies[1].wait()
+
+    def frame_of(m, tile):
+        return frames_ref[pl.ds(pl.multiple_of(tile * 128 + m * 8, 8), 8), :]
+
     second = core_ref[0] == 1
 
-    def extended_of(i, lanes):
-        own = own_ref[i, :, lanes].astype(jnp.float32)
-        zero = jnp.zeros_like(own)
-        return jnp.concatenate([jnp.where(second, own, zero), jnp.where(second, zero, own)], axis=0)
-
-    window_copy.wait()
-    for c, copy in enumerate(own_copies):
-        copy.wait()
-        fold_into(u_ref, v_ref, c * 32, range(2 * c, 2 * c + 2), 1, 512, extended_of, window_ref)
-    table_copy.wait()
+    @pl.when(jnp.logical_not(second))
+    def _():
+        fold_into(u_ref, v_ref, 0, 16, lambda t: [(15 - t + m, m) for m in range(t + 1)], frame_of, window_ref)
+
+    @pl.when(second)
+    def _():
+        fold_into(u_ref, v_ref, 0, 16, lambda t: [(m - t - 1, m) for m in range(t + 1, 16)], frame_of, window_ref)
+
+    copies[2].wait()
 
 
 def channel_kernel(
-    core_ref, own_ref, other_ref, window_ref, table_ref, list_ref, ua_ref, va_ref, out_ref, u_ref, v_ref, rows_ref
+    core_ref, frames_ref, other_ref, window_ref, table_ref, list_ref, ua_ref, va_ref, out_ref, u_ref, v_ref, rows_ref, more_ref
 ):
     second = core_ref[0] == 1
 
-    def extended_of(i, lanes):
-        own = own_ref[i, :, lanes].astype(jnp.float32)
-        other = other_ref[i, :, lanes].astype(jnp.float32)
-        return jnp.concatenate(
-            [
-                jnp.where(second, other[8:], own[:8]),
-                jnp.where(second, own[:8], own[8:]),
-                jnp.where(second, own[8:], other[:8]),
-            ],
-            axis=0,
-        )
+    def own_frame(m, tile):
+        return frames_ref[pl.ds(pl.multiple_of(tile * 128 + m * 8, 8), 8), :]
+
+    def more_frame(m, tile):
+        return more_ref[pl.ds(pl.multiple_of(tile * 64 + m * 8, 8), 8), :]
+
+    def terms_of(t):
+        return [(k, t + 1 + k) for k in range(TAPS)]
+
+    @pl.when(jnp.logical_not(second))
+    def _():
+        spread(other_ref, 0, 8, more_ref)
+
+        def frame_of(m, tile):
+            return own_frame(m, tile) if m < 16 else more_frame(m - 16, tile)
+
+        fold_into(u_ref, v_ref, 128, 8, terms_of, frame_of, window_ref)
+
+    @pl.when(second)
+    def _():
+        spread(other_ref, 8, 8, more_ref)
+
+        def frame_of(m, tile):
+            return more_frame(m, tile) if m < 8 else own_frame(m - 8, tile)
+
+        fold_into(u_ref, v_ref, 128, 8, terms_of, frame_of, window_ref)
 
     u_ref[:128, :] = ua_ref[...]
     v_ref[:128, :] = va_ref[...]
     u_ref[192:, :] = jnp.zeros((64, HALF), jnp.bfloat16)
     v_ref[192:, :] = jnp.zeros((64, HALF), jnp.bfloat16)
-    fold_into(u_ref, v_ref, 128, range(INS), 2, 512, extended_of, window_ref)
 
     low = lax.broadcasted_iota(jnp.int32, (1, 128), 1) < 64
+    whole = [
+        nt_dot(table_ref[:, parity].reshape(4 * 256, HALF), folded[...])
+        for parity, folded in enumerate((u_ref, v_ref))
+    ]
     for q in range(N_FREQ):
         halves = []
-        for parity, folded in enumerate((u_ref, v_ref)):
-            y = nt_dot(table_ref[q, parity], folded[...])
+        for parity in range(2):
+            y = whole[parity][q * 256 : (q + 1) * 256]
             re, im = y[:128, :128], y[128:, :128]
             rest = y[:128, 128:] + pltpu.roll(y[128:, 128:], 64, 1)
             first = jnp.where(low, re, pltpu.roll(im, 64, 1))
@@ -182,8 +205,14 @@
         own_kernel,
         in_specs=[pl.BlockSpec(memory_space=pltpu.SMEM), hbm, hbm, hbm],
         out_specs=[vmem] * 5,
-        out_shape=[half, half, *(pltpu.VMEM(x.shape, x.dtype) for x in (own, window, table))],
-        scratch_shapes=[pltpu.SemaphoreType.DMA((6,))],
+        out_shape=[
+            half,
+            half,
+            pltpu.VMEM((FRAME, 128), jnp.float32),
+            pltpu.VMEM(window.shape, jnp.float32),
+            pltpu.VMEM(table.shape, jnp.bfloat16),
+        ],
+        scratch_shapes=[pltpu.VMEM(own.shape, jnp.bfloat16), pltpu.SemaphoreType.DMA((3,))],
         compiler_params=pltpu.CompilerParams(vmem_limit_bytes=24 << 20),
         cost_estimate=pl.CostEstimate(flops=10_000_000, bytes_accessed=2_000_000, transcendentals=0),
         name="own",
@@ -193,7 +222,7 @@
 def channel_messages(core, own, other, lists):
     window = jnp.asarray(window_taps())
     table = jnp.asarray(fourier_halves())
-    ua, va, own, window, table = own_part(core, own, window, table)
+    ua, va, frames, window, table = own_part(core, own, window, table)
     vmem = pl.BlockSpec(memory_space=pltpu.VMEM)
     return pl.pallas_call(
         channel_kernel,
@@ -204,10 +233,11 @@
             pltpu.VMEM((256, HALF), jnp.bfloat16),
             pltpu.VMEM((256, HALF), jnp.bfloat16),
             pltpu.VMEM((N_FREQ * N_BLK * 6, 128), jnp.float32),
+            pltpu.VMEM((FRAME // 2, 128), jnp.float32),
         ],
         compiler_params=pltpu.CompilerParams(vmem_limit_bytes=32 << 20),
         name="channels",
-    )(core, own, other, window, table, lists, ua, va)
+    )(core, frames, other, window, table, lists, ua, va)
 
 
 def correlate_kernel(count_ref, got_ref, merge_ref, out_ref, rows_ref, right_all, even_all, odd_all, left_ref, right_ref):

time: 87.2 us -> 86.2 us (0.989)
  Pallas kernels: 13.2 us -> 10.2 us
  local copies, waits for them, and re-layouts: 0.01 us -> 1.89 us
    pallas_call x1, Pallas kernels: 5.48 us -> 3.46 us  [channel_messages(): pl.pallas_call(channel_kernel, in_specs=[pl.BlockSpec(memory_space=pltpu....]
    unnamed x4, local copies, waits for them, and re-layouts: 0.01 us -> 1.89 us
    pallas_call x1, Pallas kernels: 4.18 us -> 2.43 us  [own_part(): pl.pallas_call(own_kernel, in_specs=[pl.BlockSpec(memory_space=pltpu.SMEM...]
  transfers between devices with their start and end apart: 2 -> 2, of which waited for: 1 -> 1; matrix products, arithmetic and copies ran while one was open for 0% -> 0% of each run, Pallas kernels for 5% -> 3%
where the time goes in v3:
time: 86.2 us; the launch traced here: 85.9 us
  waiting for transfers between devices  46.7 us (54%)
  starting transfers between devices  26.4 us (31%)
  Pallas kernels  10.2 us (12%)
  local copies, waits for them, and re-layouts  1.89 us (2%)
    all_to_all x1, waiting for transfers between devices, shards(): lax.all_to_all(messages.reshape(N_FREQ * N_BLK, 3, 2, 128), ('z_lo', 'y',...  46.7 us
    all_to_all x1, starting transfers between devices, shards(): lax.all_to_all(messages.reshape(N_FREQ * N_BLK, 3, 2, 128), ('z_lo', 'y',...  17.5 us
    ppermute x1, starting transfers between devices, shards(): other = lax.ppermute(samples, 'core', [(0, 1), (1, 0)])  8.91 us
    pallas_call x1, Pallas kernels, visibility_tiles(): pl.pallas_call(correlate_kernel, grid=(2,), in_specs=[pl.BlockSpec(memory...  4.33 us
    pallas_call x1, Pallas kernels, channel_messages(): pl.pallas_call(channel_kernel, in_specs=[pl.BlockSpec(memory_space=pltpu....  3.46 us
    pallas_call x1, Pallas kernels, own_part(): pl.pallas_call(own_kernel, in_specs=[pl.BlockSpec(memory_space=pltpu.SMEM...  2.43 us
    unnamed x4, local copies, waits for them, and re-layouts  1.89 us
  transfers between devices with their start and end apart: 2, of which 1 were waited for; matrix products, arithmetic and copies ran while one was open for 0% of the time, Pallas kernels for 3%

profile of v3, /device:TPU:1, one launch (start us, length us, event | category | flops | bytes accessed | tf_op | source)
XLA Modules:
  0.0 85.9 jit_solution(16526618875919392213)
XLA Ops:
  0.0 0.0 copy-start.1
  0.0 8.9 %collective-permute-start = (bf16[8,16,2048]{2,1,0:T(8,128)(2,1)}, bf16[8,16,2048]{2,1,0:T(8,128)(2,1)S(1)}, u32[]{:S(2)}, u32[]{:S(2)}) collective-permute-start(bf16[8,16,2048]{2,1,0:T(8,128)(2,1)} %own_hbm.1), channel_id=1, source_target_pairs={{0,1},{1,0},{2,3},{3,2},{4,5},{5,4},{6,7},{7,6},{8,9},{9,8},{10,11... | collective-permute-start | bytes 1572872 | tf_op jit(solution)/shard_map/ppermute | solution.py:334
  8.9 2.4 %own.1 = (bf16[128,1024]{1,0:T(8,128)(2,1)S(1)}, bf16[128,1024]{1,0:T(8,128)(2,1)S(1)}, f32[2048,128]{1,0:T(8,128)S(1)}, f32[16,2048]{1,0:T(8,128)S(1)}, bf16[4,2,256,1024]{3,2,1,0:T(8,128)(2,1)S(1)}) custom-call(s32[1]{0:T(128)} %bitcast.core_ref, bf16[8,16,2048]{2,1,0:T(8,128)(2,1)} %own_hbm.1, f32[16,2048]{1,0:T(8,128)} %constant.10.clone.window_hbm, ...), custom_call_target="tpu_custom_call" | custom-call | flops 10000000 | bytes 2000000 | tf_op jit(solution)/shard_map/own/pallas_call | solution.py:204
  11.4 0.0 collective-permute-done.other_ref
  11.4 0.0 copy-done.1
  11.4 3.5 %channels.1 = bf16[3072,128]{1,0:T(8,128)(2,1)} custom-call(s32[1]{0:T(128)} %bitcast.core_ref, f32[2048,128]{1,0:T(8,128)S(1)} %get-tuple-element.10.frames_ref, bf16[8,16,2048]{2,1,0:T(8,128)(2,1)S(1)} %collective-permute-done.other_ref, f32[16,2048]{1,0:T(8,128)S(1)} %get-tuple-element.11.window_ref, ...), custom_call_target="tpu_custom_call" | custom-call | tf_op jit(solution)/shard_map/channels/pallas_call | solution.py:227
  14.8 17.5 %all-to-all-start = ((bf16[512,3,2,128]{3,2,1,0:T(2,128)(2,1)}), bf16[512,3,2,128]{3,2,1,0:T(2,128)(2,1)S(1)}, u32[]{:S(2)}, u32[]{:S(2)}) async-start(bf16[512,3,2,128]{3,2,1,0:T(2,128)(2,1)} %bitcast.2), calls=%async_computation | async-start | bytes 1572864 | tf_op jit(solution)/shard_map/all_to_all | solution.py:337
  33.0 46.7 %all-to-all-done = bf16[512,3,2,128]{3,2,1,0:T(2,128)(2,1)S(1)} async-done(((bf16[512,3,2,128]{3,2,1,0:T(2,128)(2,1)}), bf16[512,3,2,128]{3,2,1,0:T(2,128)(2,1)S(1)}, u32[]{:S(2)}, u32[]{:S(2)}) %all-to-all-start) | async-done | bytes 786464 | tf_op jit(solution)/shard_map/all_to_all | solution.py:337
  79.7 0.0 copy-start
  79.7 1.9 %copy-done = bf16[6144,256]{1,0:T(8,128)(2,1)S(1)} copy-done((bf16[6144,256]{1,0:T(8,128)(2,1)S(1)}, bf16[6144,256]{1,0:T(8,128)(2,1)}, u32[]{:S(2)}) %copy-start) | copy-done | bytes 3145752
  81.6 4.3 %correlate.1 = bf16[2,136,64,128]{3,2,1,0:T(8,128)(2,1)} custom-call(s32[1,1]{1,0:T(1,128)S(6)} %copy.8.count_ref, bf16[3072,128]{1,0:T(8,128)(2,1)S(1)} %bitcast.9, bf16[6144,256]{1,0:T(8,128)(2,1)S(1)} %copy-done), custom_call_target="tpu_custom_call" | custom-call | tf_op jit(solution)/shard_map/correlate/pallas_call | solution.py:309
Async XLA Ops:
  0.0 11.4 %copy-start.1 = (s32[4,128,2]{1,2,0:T(2,128)S(1)}, s32[4,128,2]{1,2,0:T(2,128)}, u32[]{:S(2)}) copy-start(s32[4,128,2]{1,2,0:T(2,128)} %param.7) | copy-start | bytes 12292
  0.0 11.4 %collective-permute-start = (bf16[8,16,2048]{2,1,0:T(8,128)(2,1)}, bf16[8,16,2048]{2,1,0:T(8,128)(2,1)S(1)}, u32[]{:S(2)}, u32[]{:S(2)}) collective-permute-start(bf16[8,16,2048]{2,1,0:T(8,128)(2,1)} %own_hbm.1), channel_id=1, source_target_pairs={{0,1},{1,0},{2,3},{3,2},{4,5},{5,4},{6,7},{7,6},{8,9},{9,8},{10,11... | collective-permute-start | bytes 1572872 | tf_op jit(solution)/shard_map/ppermute | solution.py:334
  14.8 64.9 %all-to-all-start = ((bf16[512,3,2,128]{3,2,1,0:T(2,128)(2,1)}), bf16[512,3,2,128]{3,2,1,0:T(2,128)(2,1)S(1)}, u32[]{:S(2)}, u32[]{:S(2)}) async-start(bf16[512,3,2,128]{3,2,1,0:T(2,128)(2,1)} %bitcast.2), calls=%async_computation | async-start | bytes 1572864 | tf_op jit(solution)/shard_map/all_to_all | solution.py:337
  79.7 1.9 %copy-start = (bf16[6144,256]{1,0:T(8,128)(2,1)S(1)}, bf16[6144,256]{1,0:T(8,128)(2,1)}, u32[]{:S(2)}) copy-start(bf16[6144,256]{1,0:T(8,128)(2,1)} %constant.12.clone.merge_ref) | copy-start | bytes 9437188

commit v4 on v3

--- a/solution.py
+++ b/solution.py
@@ -19,7 +19,7 @@
 N_FREQ = 4
 TILES = 16
 PAIRS = 136
-GROUPS = ((0, 1, 2),) * 4
+GROUPS = ((0, 1), (0, 1), (1, 2), (1, 2))
 
 
 def window_taps():
@@ -43,7 +43,7 @@
 def message_lane(core, i, t, r):
     own = t - 8 * core
     if 0 <= own < 16:
-        return own // 8 * 256 + 64 * r + own % 8 * 8 + i
+        return i // 4 * 256 + 64 * r + own * 4 + i % 4
     return 128 + 64 * r + t % 8 * 8 + i
 
 
@@ -76,7 +76,14 @@
             into_ref[pl.ds(tile * frames * 8 + i, frames, stride=8), :] = values[first : first + frames]
 
 
-def fold_into(u_ref, v_ref, row, outputs, terms_of, frame_of, window_ref):
+def by_fours(rows):
+    first = lax.broadcasted_iota(jnp.int32, (8, 1), 0) < 4
+    low = [jnp.where(first, a, pltpu.roll(b, 4, 0)) for a, b in zip(rows[::2], rows[1::2])]
+    high = [jnp.where(first, pltpu.roll(a, 4, 0), b) for a, b in zip(rows[::2], rows[1::2])]
+    return low + high
+
+
+def fold_into(u_ref, v_ref, row, outputs, terms_of, frame_of, window_ref, order=list):
     def one(tile, carry):
         parts = []
         for half in (tile, tile + HALF // 128):
@@ -93,11 +100,12 @@
                 totals.append(total)
             parts.append(totals)
         lanes = pl.ds(pl.multiple_of(tile * 128, 128), 128)
+        sums = order([low + high for low, high in zip(*parts)])
+        differences = order([low - high for low, high in zip(*parts)])
         for t in range(0, outputs, 2):
-            low = jnp.concatenate(parts[0][t : t + 2], axis=0)
-            high = jnp.concatenate(parts[1][t : t + 2], axis=0)
-            u_ref[row + t * 8 : row + t * 8 + 16, lanes] = (low + high).astype(jnp.bfloat16)
-            v_ref[row + t * 8 : row + t * 8 + 16, lanes] = (low - high).astype(jnp.bfloat16)
+            rows = slice(row + t * 8, row + t * 8 + 16)
+            u_ref[rows, lanes] = jnp.concatenate(sums[t : t + 2], axis=0).astype(jnp.bfloat16)
+            v_ref[rows, lanes] = jnp.concatenate(differences[t : t + 2], axis=0).astype(jnp.bfloat16)
         return carry
 
     lax.fori_loop(0, HALF // 128, one, 0)
@@ -122,11 +130,11 @@
 
     @pl.when(jnp.logical_not(second))
     def _():
-        fold_into(u_ref, v_ref, 0, 16, lambda t: [(15 - t + m, m) for m in range(t + 1)], frame_of, window_ref)
+        fold_into(u_ref, v_ref, 0, 16, lambda t: [(15 - t + m, m) for m in range(t + 1)], frame_of, window_ref, by_fours)
 
     @pl.when(second)
     def _():
-        fold_into(u_ref, v_ref, 0, 16, lambda t: [(m - t - 1, m) for m in range(t + 1, 16)], frame_of, window_ref)
+        fold_into(u_ref, v_ref, 0, 16, lambda t: [(m - t - 1, m) for m in range(t + 1, 16)], frame_of, window_ref, by_fours)
 
     copies[2].wait()
 

time: 86.2 us -> 84 us (0.974)
  local copies, waits for them, and re-layouts: 1.89 us -> 0.01 us
    unnamed x4, local copies, waits for them, and re-layouts: 1.89 us -> 0.01 us
where the time goes in v4:
time: 84 us; the launch traced here: 83.8 us
  waiting for transfers between devices  46.7 us (56%)
  starting transfers between devices  26.4 us (31%)
  Pallas kernels  9.99 us (12%)
    all_to_all x1, waiting for transfers between devices, shards(): lax.all_to_all(messages.reshape(N_FREQ * N_BLK, 3, 2, 128), ('z_lo', 'y',...  46.7 us
    all_to_all x1, starting transfers between devices, shards(): lax.all_to_all(messages.reshape(N_FREQ * N_BLK, 3, 2, 128), ('z_lo', 'y',...  17.5 us
    ppermute x1, starting transfers between devices, shards(): other = lax.ppermute(samples, 'core', [(0, 1), (1, 0)])  8.91 us
    pallas_call x1, Pallas kernels, visibility_tiles(): pl.pallas_call(correlate_kernel, grid=(2,), in_specs=[pl.BlockSpec(memory...  4.1 us
    pallas_call x1, Pallas kernels, channel_messages(): pl.pallas_call(channel_kernel, in_specs=[pl.BlockSpec(memory_space=pltpu....  3.46 us
    pallas_call x1, Pallas kernels, own_part(): pl.pallas_call(own_kernel, in_specs=[pl.BlockSpec(memory_space=pltpu.SMEM...  2.43 us
  transfers between devices with their start and end apart: 2, of which 1 were waited for; matrix products, arithmetic and copies ran while one was open for 0% of the time, Pallas kernels for 3%

profile of v4, /device:TPU:1, one launch (start us, length us, event | category | flops | bytes accessed | tf_op | source)
XLA Modules:
  0.0 83.8 jit_solution(17617013076685845855)
XLA Ops:
  0.0 0.0 copy-start.1
  0.0 8.9 %collective-permute-start = (bf16[8,16,2048]{2,1,0:T(8,128)(2,1)}, bf16[8,16,2048]{2,1,0:T(8,128)(2,1)S(1)}, u32[]{:S(2)}, u32[]{:S(2)}) collective-permute-start(bf16[8,16,2048]{2,1,0:T(8,128)(2,1)} %own_hbm.1), channel_id=1, source_target_pairs={{0,1},{1,0},{2,3},{3,2},{4,5},{5,4},{6,7},{7,6},{8,9},{9,8},{10,11... | collective-permute-start | bytes 1572872 | tf_op jit(solution)/shard_map/ppermute | solution.py:342
  8.9 2.4 %own.1 = (bf16[128,1024]{1,0:T(8,128)(2,1)S(1)}, bf16[128,1024]{1,0:T(8,128)(2,1)S(1)}, f32[2048,128]{1,0:T(8,128)S(1)}, f32[16,2048]{1,0:T(8,128)S(1)}, bf16[4,2,256,1024]{3,2,1,0:T(8,128)(2,1)S(1)}) custom-call(s32[1]{0:T(128)} %bitcast.core_ref, bf16[8,16,2048]{2,1,0:T(8,128)(2,1)} %own_hbm.1, f32[16,2048]{1,0:T(8,128)} %constant.10.clone.window_hbm, ...), custom_call_target="tpu_custom_call" | custom-call | flops 10000000 | bytes 2000000 | tf_op jit(solution)/shard_map/own/pallas_call | solution.py:212
  11.4 0.0 collective-permute-done.other_ref
  11.4 0.0 copy-done.1
  11.4 0.0 copy-start
  11.4 3.5 %channels.1 = bf16[3072,128]{1,0:T(8,128)(2,1)} custom-call(s32[1]{0:T(128)} %bitcast.core_ref, f32[2048,128]{1,0:T(8,128)S(1)} %get-tuple-element.10.frames_ref, bf16[8,16,2048]{2,1,0:T(8,128)(2,1)S(1)} %collective-permute-done.other_ref, f32[16,2048]{1,0:T(8,128)S(1)} %get-tuple-element.11.window_ref, ...), custom_call_target="tpu_custom_call" | custom-call | tf_op jit(solution)/shard_map/channels/pallas_call | solution.py:235
  14.9 17.5 %all-to-all-start = ((bf16[512,3,2,128]{3,2,1,0:T(2,128)(2,1)}), bf16[512,3,2,128]{3,2,1,0:T(2,128)(2,1)S(1)}, u32[]{:S(2)}, u32[]{:S(2)}) async-start(bf16[512,3,2,128]{3,2,1,0:T(2,128)(2,1)} %bitcast.2), calls=%async_computation | async-start | bytes 1572864 | tf_op jit(solution)/shard_map/all_to_all | solution.py:345
  33.0 46.7 %all-to-all-done = bf16[512,3,2,128]{3,2,1,0:T(2,128)(2,1)S(1)} async-done(((bf16[512,3,2,128]{3,2,1,0:T(2,128)(2,1)}), bf16[512,3,2,128]{3,2,1,0:T(2,128)(2,1)S(1)}, u32[]{:S(2)}, u32[]{:S(2)}) %all-to-all-start) | async-done | bytes 786464 | tf_op jit(solution)/shard_map/all_to_all | solution.py:345
  79.7 0.0 copy-done
  79.7 4.1 %correlate.1 = bf16[2,136,64,128]{3,2,1,0:T(8,128)(2,1)} custom-call(s32[1,1]{1,0:T(1,128)S(6)} %copy.8.count_ref, bf16[3072,128]{1,0:T(8,128)(2,1)S(1)} %bitcast.9, bf16[4096,256]{1,0:T(8,128)(2,1)S(1)} %copy-done), custom_call_target="tpu_custom_call" | custom-call | tf_op jit(solution)/shard_map/correlate/pallas_call | solution.py:317
Async XLA Ops:
  0.0 11.4 %copy-start.1 = (s32[4,128,2]{1,2,0:T(2,128)S(1)}, s32[4,128,2]{1,2,0:T(2,128)}, u32[]{:S(2)}) copy-start(s32[4,128,2]{1,2,0:T(2,128)} %param.7) | copy-start | bytes 12292
  0.0 11.4 %collective-permute-start = (bf16[8,16,2048]{2,1,0:T(8,128)(2,1)}, bf16[8,16,2048]{2,1,0:T(8,128)(2,1)S(1)}, u32[]{:S(2)}, u32[]{:S(2)}) collective-permute-start(bf16[8,16,2048]{2,1,0:T(8,128)(2,1)} %own_hbm.1), channel_id=1, source_target_pairs={{0,1},{1,0},{2,3},{3,2},{4,5},{5,4},{6,7},{7,6},{8,9},{9,8},{10,11... | collective-permute-start | bytes 1572872 | tf_op jit(solution)/shard_map/ppermute | solution.py:342
  11.4 68.4 %copy-start = (bf16[4096,256]{1,0:T(8,128)(2,1)S(1)}, bf16[4096,256]{1,0:T(8,128)(2,1)}, u32[]{:S(2)}) copy-start(bf16[4096,256]{1,0:T(8,128)(2,1)} %constant.12.clone.merge_ref) | copy-start | bytes 6291460
  14.9 64.9 %all-to-all-start = ((bf16[512,3,2,128]{3,2,1,0:T(2,128)(2,1)}), bf16[512,3,2,128]{3,2,1,0:T(2,128)(2,1)S(1)}, u32[]{:S(2)}, u32[]{:S(2)}) async-start(bf16[512,3,2,128]{3,2,1,0:T(2,128)(2,1)} %bitcast.2), calls=%async_computation | async-start | bytes 1572864 | tf_op jit(solution)/shard_map/all_to_all | solution.py:345

commit v5 on v4

--- a/solution.py
+++ b/solution.py
@@ -140,7 +140,7 @@
 
 
 def channel_kernel(
-    core_ref, frames_ref, other_ref, window_ref, table_ref, list_ref, ua_ref, va_ref, out_ref, u_ref, v_ref, rows_ref, more_ref
+    core_ref, frames_ref, other_ref, window_ref, table_ref, list_ref, ua_ref, va_ref, out_hbm, u_ref, v_ref, rows_ref, more_ref, out_ref, sems
 ):
     second = core_ref[0] == 1
 
@@ -181,6 +181,7 @@
         nt_dot(table_ref[:, parity].reshape(4 * 256, HALF), folded[...])
         for parity, folded in enumerate((u_ref, v_ref))
     ]
+    copies = []
     for q in range(N_FREQ):
         halves = []
         for parity in range(2):
@@ -198,10 +199,15 @@
         picked = jnp.dot(picks.T.astype(jnp.bfloat16), spectra, preferred_element_type=jnp.float32)
         for tile in range(3):
             for slot in range(2):
-                rows_ref[pl.ds(q * 6 + tile * 2 + slot, N_BLK, stride=N_FREQ * 6), :] = picked[
+                rows_ref[pl.ds(tile * 2 + slot, N_BLK, stride=6), :] = picked[
                     slot * N_BLK : (slot + 1) * N_BLK, tile * 128 : (tile + 1) * 128
                 ]
-    out_ref[...] = rows_ref[...].astype(jnp.bfloat16)
+        own_rows = slice(q * N_BLK * 6, (q + 1) * N_BLK * 6)
+        out_ref[own_rows, :] = rows_ref[...].astype(jnp.bfloat16)
+        copies.append(pltpu.make_async_copy(out_ref.at[own_rows], out_hbm.at[own_rows], sems.at[q]))
+        copies[-1].start()
+    for copy in copies:
+        copy.wait()
 
 
 def own_part(core, own, window, table):
@@ -235,13 +241,15 @@
     return pl.pallas_call(
         channel_kernel,
         in_specs=[pl.BlockSpec(memory_space=pltpu.SMEM)] + [vmem] * 7,
-        out_specs=vmem,
+        out_specs=pl.BlockSpec(memory_space=pltpu.HBM),
         out_shape=jax.ShapeDtypeStruct((N_FREQ * N_BLK * 6, 128), jnp.bfloat16),
         scratch_shapes=[
             pltpu.VMEM((256, HALF), jnp.bfloat16),
             pltpu.VMEM((256, HALF), jnp.bfloat16),
-            pltpu.VMEM((N_FREQ * N_BLK * 6, 128), jnp.float32),
+            pltpu.VMEM((N_BLK * 6, 128), jnp.float32),
             pltpu.VMEM((FRAME // 2, 128), jnp.float32),
+            pltpu.VMEM((N_FREQ * N_BLK * 6, 128), jnp.bfloat16),
+            pltpu.SemaphoreType.DMA((N_FREQ,)),
         ],
         compiler_params=pltpu.CompilerParams(vmem_limit_bytes=32 << 20),
         name="channels",
@@ -258,9 +266,9 @@
         sources = {}
         for f in range(N_FREQ):
             for tile in range(3):
-                start = f * 6 + tile * 2
+                start = f * N_BLK * 6 + tile * 2
                 sources[f, tile] = jnp.concatenate(
-                    [rows_ref[pl.ds(start + j, N_BLK, stride=N_FREQ * 6), :] for j in range(2)], axis=0
+                    [rows_ref[pl.ds(start + j, N_BLK, stride=6), :] for j in range(2)], axis=0
                 ).astype(jnp.bfloat16)
         base = 0
         for pair, tiles in enumerate(GROUPS):
@@ -343,7 +351,7 @@
     lists = channel_lists.transpose(0, 2, 1)
     messages = channel_messages(core, samples, other, lists)
     got = lax.all_to_all(
-        messages.reshape(N_FREQ * N_BLK, 3, 2, 128), ("z_lo", "y", "x", "z_hi", "core"), 0, 0, tiled=True
+        messages.reshape(N_FREQ * N_BLK, 3, 2, 128), ("z_hi", "core", "z_lo", "y", "x"), 0, 0, tiled=True
     ).reshape(N_FREQ * N_BLK * 6, 128)
     tiles = visibility_tiles(channel_counts, got)
     tiles = tiles.reshape(2, PAIRS, 32, 2, 128).transpose(0, 1, 3, 2, 4)

time: 84 us -> 83.4 us (level)
  no operation moved by 1% of the time
where the time goes in v5:
time: 83.4 us; the launch traced here: 83.2 us
  waiting for transfers between devices  46.3 us (56%)
  starting transfers between devices  26.5 us (32%)
  Pallas kernels  9.72 us (12%)
    all_to_all x1, waiting for transfers between devices, shards(): lax.all_to_all(messages.reshape(N_FREQ * N_BLK, 3, 2, 128), ('z_hi', 'cor...  46.3 us
    all_to_all x1, starting transfers between devices, shards(): lax.all_to_all(messages.reshape(N_FREQ * N_BLK, 3, 2, 128), ('z_hi', 'cor...  17.5 us
    ppermute x1, starting transfers between devices, shards(): other = lax.ppermute(samples, 'core', [(0, 1), (1, 0)])  8.91 us
    pallas_call x1, Pallas kernels, visibility_tiles(): pl.pallas_call(correlate_kernel, grid=(2,), in_specs=[pl.BlockSpec(memory...  4.02 us
    pallas_call x1, Pallas kernels, channel_messages(): pl.pallas_call(channel_kernel, in_specs=[pl.BlockSpec(memory_space=pltpu....  3.28 us
    pallas_call x1, Pallas kernels, own_part(): pl.pallas_call(own_kernel, in_specs=[pl.BlockSpec(memory_space=pltpu.SMEM...  2.43 us
  transfers between devices with their start and end apart: 2, of which 1 were waited for; matrix products, arithmetic and copies ran while one was open for 0% of the time, Pallas kernels for 3%

profile of v5, /device:TPU:1, one launch (start us, length us, event | category | flops | bytes accessed | tf_op | source)
XLA Modules:
  0.0 83.2 jit_solution(1894418917011747018)
XLA Ops:
  0.0 0.0 copy-start.1
  0.0 8.9 %collective-permute-start = (bf16[8,16,2048]{2,1,0:T(8,128)(2,1)}, bf16[8,16,2048]{2,1,0:T(8,128)(2,1)S(1)}, u32[]{:S(2)}, u32[]{:S(2)}) collective-permute-start(bf16[8,16,2048]{2,1,0:T(8,128)(2,1)} %own_hbm.1), channel_id=1, source_target_pairs={{0,1},{1,0},{2,3},{3,2},{4,5},{5,4},{6,7},{7,6},{8,9},{9,8},{10,11... | collective-permute-start | bytes 1572872 | tf_op jit(solution)/shard_map/ppermute | solution.py:350
  8.9 2.4 %own.1 = (bf16[128,1024]{1,0:T(8,128)(2,1)S(1)}, bf16[128,1024]{1,0:T(8,128)(2,1)S(1)}, f32[2048,128]{1,0:T(8,128)S(1)}, f32[16,2048]{1,0:T(8,128)S(1)}, bf16[4,2,256,1024]{3,2,1,0:T(8,128)(2,1)S(1)}) custom-call(s32[1]{0:T(128)} %bitcast.core_ref, bf16[8,16,2048]{2,1,0:T(8,128)(2,1)} %own_hbm.1, f32[16,2048]{1,0:T(8,128)} %constant.10.clone.window_hbm, ...), custom_call_target="tpu_custom_call" | custom-call | flops 10000000 | bytes 2000000 | tf_op jit(solution)/shard_map/own/pallas_call | solution.py:218
  11.4 0.0 collective-permute-done.other_ref
  11.4 0.0 copy-done.1
  11.4 0.0 copy-start
  11.4 3.3 %channels.1 = bf16[3072,128]{1,0:T(8,128)(2,1)} custom-call(s32[1]{0:T(128)} %bitcast.core_ref, f32[2048,128]{1,0:T(8,128)S(1)} %get-tuple-element.10.frames_ref, bf16[8,16,2048]{2,1,0:T(8,128)(2,1)S(1)} %collective-permute-done.other_ref, f32[16,2048]{1,0:T(8,128)S(1)} %get-tuple-element.11.window_ref, ...), custom_call_target="tpu_custom_call" | custom-call | tf_op jit(solution)/shard_map/channels/pallas_call | solution.py:241
  14.7 17.5 %all-to-all-start = ((bf16[512,3,2,128]{3,2,1,0:T(2,128)(2,1)}), bf16[512,3,2,128]{3,2,1,0:T(2,128)(2,1)S(1)}, u32[]{:S(2)}, u32[]{:S(2)}) async-start(bf16[512,3,2,128]{3,2,1,0:T(2,128)(2,1)} %bitcast.2), calls=%async_computation | async-start | bytes 1572864 | tf_op jit(solution)/shard_map/all_to_all | solution.py:353
  32.9 46.3 %all-to-all-done = bf16[512,3,2,128]{3,2,1,0:T(2,128)(2,1)S(1)} async-done(((bf16[512,3,2,128]{3,2,1,0:T(2,128)(2,1)}), bf16[512,3,2,128]{3,2,1,0:T(2,128)(2,1)S(1)}, u32[]{:S(2)}, u32[]{:S(2)}) %all-to-all-start) | async-done | bytes 786464 | tf_op jit(solution)/shard_map/all_to_all | solution.py:353
  79.2 0.0 copy-done
  79.2 4.0 %correlate.1 = bf16[2,136,64,128]{3,2,1,0:T(8,128)(2,1)} custom-call(s32[1,1]{1,0:T(1,128)S(6)} %copy.8.count_ref, bf16[3072,128]{1,0:T(8,128)(2,1)S(1)} %bitcast.9, bf16[4096,256]{1,0:T(8,128)(2,1)S(1)} %copy-done), custom_call_target="tpu_custom_call" | custom-call | tf_op jit(solution)/shard_map/correlate/pallas_call | solution.py:325
Async XLA Ops:
  0.0 11.4 %copy-start.1 = (s32[4,128,2]{1,2,0:T(2,128)S(1)}, s32[4,128,2]{1,2,0:T(2,128)}, u32[]{:S(2)}) copy-start(s32[4,128,2]{1,2,0:T(2,128)} %param.7) | copy-start | bytes 12292
  0.0 11.4 %collective-permute-start = (bf16[8,16,2048]{2,1,0:T(8,128)(2,1)}, bf16[8,16,2048]{2,1,0:T(8,128)(2,1)S(1)}, u32[]{:S(2)}, u32[]{:S(2)}) collective-permute-start(bf16[8,16,2048]{2,1,0:T(8,128)(2,1)} %own_hbm.1), channel_id=1, source_target_pairs={{0,1},{1,0},{2,3},{3,2},{4,5},{5,4},{6,7},{7,6},{8,9},{9,8},{10,11... | collective-permute-start | bytes 1572872 | tf_op jit(solution)/shard_map/ppermute | solution.py:350
  11.4 67.8 %copy-start = (bf16[4096,256]{1,0:T(8,128)(2,1)S(1)}, bf16[4096,256]{1,0:T(8,128)(2,1)}, u32[]{:S(2)}) copy-start(bf16[4096,256]{1,0:T(8,128)(2,1)} %constant.12.clone.merge_ref) | copy-start | bytes 6291460
  14.7 64.5 %all-to-all-start = ((bf16[512,3,2,128]{3,2,1,0:T(2,128)(2,1)}), bf16[512,3,2,128]{3,2,1,0:T(2,128)(2,1)S(1)}, u32[]{:S(2)}, u32[]{:S(2)}) async-start(bf16[512,3,2,128]{3,2,1,0:T(2,128)(2,1)} %bitcast.2), calls=%async_computation | async-start | bytes 1572864 | tf_op jit(solution)/shard_map/all_to_all | solution.py:353

commit v6 on v5

--- a/solution.py
+++ b/solution.py
@@ -108,7 +108,7 @@
             v_ref[rows, lanes] = jnp.concatenate(differences[t : t + 2], axis=0).astype(jnp.bfloat16)
         return carry
 
-    lax.fori_loop(0, HALF // 128, one, 0)
+    lax.fori_loop(0, HALF // 128, one, 0, unroll=2)
 
 
 def own_kernel(core_ref, own_hbm, window_hbm, table_hbm, u_ref, v_ref, frames_ref, window_ref, table_ref, own_ref, sems):
@@ -202,7 +202,8 @@
                 rows_ref[pl.ds(tile * 2 + slot, N_BLK, stride=6), :] = picked[
                     slot * N_BLK : (slot + 1) * N_BLK, tile * 128 : (tile + 1) * 128
                 ]
-        own_rows = slice(q * N_BLK * 6, (q + 1) * N_BLK * 6)
+        place_q = q % 2 * 2 + q // 2
+        own_rows = slice(place_q * N_BLK * 6, (place_q + 1) * N_BLK * 6)
         out_ref[own_rows, :] = rows_ref[...].astype(jnp.bfloat16)
         copies.append(pltpu.make_async_copy(out_ref.at[own_rows], out_hbm.at[own_rows], sems.at[q]))
         copies[-1].start()
@@ -266,7 +267,7 @@
         sources = {}
         for f in range(N_FREQ):
             for tile in range(3):
-                start = f * N_BLK * 6 + tile * 2
+                start = (f % 2 * 2 + f // 2) * N_BLK * 6 + tile * 2
                 sources[f, tile] = jnp.concatenate(
                     [rows_ref[pl.ds(start + j, N_BLK, stride=6), :] for j in range(2)], axis=0
                 ).astype(jnp.bfloat16)
@@ -351,7 +352,7 @@
     lists = channel_lists.transpose(0, 2, 1)
     messages = channel_messages(core, samples, other, lists)
     got = lax.all_to_all(
-        messages.reshape(N_FREQ * N_BLK, 3, 2, 128), ("z_hi", "core", "z_lo", "y", "x"), 0, 0, tiled=True
+        messages.reshape(N_FREQ * N_BLK, 3, 2, 128), ("core", "z_hi", "z_lo", "y", "x"), 0, 0, tiled=True
     ).reshape(N_FREQ * N_BLK * 6, 128)
     tiles = visibility_tiles(channel_counts, got)
     tiles = tiles.reshape(2, PAIRS, 32, 2, 128).transpose(0, 1, 3, 2, 4)

time: 83.4 us -> 81.5 us (0.977)
  waiting for transfers between devices: 46.3 us -> 44.3 us
    all_to_all x1, waiting for transfers between devices: 46.3 us -> 44.3 us  [shards(): lax.all_to_all(messages.reshape(N_FREQ * N_BLK, 3, 2, 128), ('core', 'z_h...]
where the time goes in v6:
time: 81.5 us; the launch traced here: 81.2 us
  waiting for transfers between devices  44.3 us (54%)
  starting transfers between devices  26.5 us (33%)
  Pallas kernels  9.71 us (12%)
    all_to_all x1, waiting for transfers between devices, shards(): lax.all_to_all(messages.reshape(N_FREQ * N_BLK, 3, 2, 128), ('core', 'z_h...  44.3 us
    all_to_all x1, starting transfers between devices, shards(): lax.all_to_all(messages.reshape(N_FREQ * N_BLK, 3, 2, 128), ('core', 'z_h...  17.5 us
    ppermute x1, starting transfers between devices, shards(): other = lax.ppermute(samples, 'core', [(0, 1), (1, 0)])  8.91 us
    pallas_call x1, Pallas kernels, visibility_tiles(): pl.pallas_call(correlate_kernel, grid=(2,), in_specs=[pl.BlockSpec(memory...  4.03 us
    pallas_call x1, Pallas kernels, channel_messages(): pl.pallas_call(channel_kernel, in_specs=[pl.BlockSpec(memory_space=pltpu....  3.25 us
    pallas_call x1, Pallas kernels, own_part(): pl.pallas_call(own_kernel, in_specs=[pl.BlockSpec(memory_space=pltpu.SMEM...  2.43 us
  transfers between devices with their start and end apart: 2, of which 1 were waited for; matrix products, arithmetic and copies ran while one was open for 0% of the time, Pallas kernels for 3%

profile of v6, /device:TPU:1, one launch (start us, length us, event | category | flops | bytes accessed | tf_op | source)
XLA Modules:
  0.0 81.2 jit_solution(11796267651552908222)
XLA Ops:
  0.0 0.0 copy-start.1
  0.0 8.9 %collective-permute-start = (bf16[8,16,2048]{2,1,0:T(8,128)(2,1)}, bf16[8,16,2048]{2,1,0:T(8,128)(2,1)S(1)}, u32[]{:S(2)}, u32[]{:S(2)}) collective-permute-start(bf16[8,16,2048]{2,1,0:T(8,128)(2,1)} %own_hbm.1), channel_id=1, source_target_pairs={{0,1},{1,0},{2,3},{3,2},{4,5},{5,4},{6,7},{7,6},{8,9},{9,8},{10,11... | collective-permute-start | bytes 1572872 | tf_op jit(solution)/shard_map/ppermute | solution.py:351
  8.9 2.4 %own.1 = (bf16[128,1024]{1,0:T(8,128)(2,1)S(1)}, bf16[128,1024]{1,0:T(8,128)(2,1)S(1)}, f32[2048,128]{1,0:T(8,128)S(1)}, f32[16,2048]{1,0:T(8,128)S(1)}, bf16[4,2,256,1024]{3,2,1,0:T(8,128)(2,1)S(1)}) custom-call(s32[1]{0:T(128)} %bitcast.core_ref, bf16[8,16,2048]{2,1,0:T(8,128)(2,1)} %own_hbm.1, f32[16,2048]{1,0:T(8,128)} %constant.10.clone.window_hbm, ...), custom_call_target="tpu_custom_call" | custom-call | flops 10000000 | bytes 2000000 | tf_op jit(solution)/shard_map/own/pallas_call | solution.py:219
  11.4 0.0 collective-permute-done.other_ref
  11.4 0.0 copy-done.1
  11.4 0.0 copy-start
  11.4 3.3 %channels.1 = bf16[3072,128]{1,0:T(8,128)(2,1)} custom-call(s32[1]{0:T(128)} %bitcast.core_ref, f32[2048,128]{1,0:T(8,128)S(1)} %get-tuple-element.10.frames_ref, bf16[8,16,2048]{2,1,0:T(8,128)(2,1)S(1)} %collective-permute-done.other_ref, f32[16,2048]{1,0:T(8,128)S(1)} %get-tuple-element.11.window_ref, ...), custom_call_target="tpu_custom_call" | custom-call | tf_op jit(solution)/shard_map/channels/pallas_call | solution.py:242
  14.7 17.5 %all-to-all-start = ((bf16[512,3,2,128]{3,2,1,0:T(2,128)(2,1)}), bf16[512,3,2,128]{3,2,1,0:T(2,128)(2,1)S(1)}, u32[]{:S(2)}, u32[]{:S(2)}) async-start(bf16[512,3,2,128]{3,2,1,0:T(2,128)(2,1)} %bitcast.2), calls=%async_computation | async-start | bytes 1572864 | tf_op jit(solution)/shard_map/all_to_all | solution.py:354
  32.9 44.3 %all-to-all-done = bf16[512,3,2,128]{3,2,1,0:T(2,128)(2,1)S(1)} async-done(((bf16[512,3,2,128]{3,2,1,0:T(2,128)(2,1)}), bf16[512,3,2,128]{3,2,1,0:T(2,128)(2,1)S(1)}, u32[]{:S(2)}, u32[]{:S(2)}) %all-to-all-start) | async-done | bytes 786464 | tf_op jit(solution)/shard_map/all_to_all | solution.py:354
  77.2 0.0 copy-done
  77.2 4.0 %correlate.1 = bf16[2,136,64,128]{3,2,1,0:T(8,128)(2,1)} custom-call(s32[1,1]{1,0:T(1,128)S(6)} %copy.8.count_ref, bf16[3072,128]{1,0:T(8,128)(2,1)S(1)} %bitcast.9, bf16[4096,256]{1,0:T(8,128)(2,1)S(1)} %copy-done), custom_call_target="tpu_custom_call" | custom-call | tf_op jit(solution)/shard_map/correlate/pallas_call | solution.py:326
Async XLA Ops:
  0.0 11.4 %copy-start.1 = (s32[4,128,2]{1,2,0:T(2,128)S(1)}, s32[4,128,2]{1,2,0:T(2,128)}, u32[]{:S(2)}) copy-start(s32[4,128,2]{1,2,0:T(2,128)} %param.7) | copy-start | bytes 12292
  0.0 11.4 %collective-permute-start = (bf16[8,16,2048]{2,1,0:T(8,128)(2,1)}, bf16[8,16,2048]{2,1,0:T(8,128)(2,1)S(1)}, u32[]{:S(2)}, u32[]{:S(2)}) collective-permute-start(bf16[8,16,2048]{2,1,0:T(8,128)(2,1)} %own_hbm.1), channel_id=1, source_target_pairs={{0,1},{1,0},{2,3},{3,2},{4,5},{5,4},{6,7},{7,6},{8,9},{9,8},{10,11... | collective-permute-start | bytes 1572872 | tf_op jit(solution)/shard_map/ppermute | solution.py:351
  11.4 65.8 %copy-start = (bf16[4096,256]{1,0:T(8,128)(2,1)S(1)}, bf16[4096,256]{1,0:T(8,128)(2,1)}, u32[]{:S(2)}) copy-start(bf16[4096,256]{1,0:T(8,128)(2,1)} %constant.12.clone.merge_ref) | copy-start | bytes 6291460
  14.7 62.5 %all-to-all-start = ((bf16[512,3,2,128]{3,2,1,0:T(2,128)(2,1)}), bf16[512,3,2,128]{3,2,1,0:T(2,128)(2,1)S(1)}, u32[]{:S(2)}, u32[]{:S(2)}) async-start(bf16[512,3,2,128]{3,2,1,0:T(2,128)(2,1)} %bitcast.2), calls=%async_computation | async-start | bytes 1572864 | tf_op jit(solution)/shard_map/all_to_all | solution.py:354

commit v7 on v6

--- a/solution.py
+++ b/solution.py
@@ -108,7 +108,7 @@
             v_ref[rows, lanes] = jnp.concatenate(differences[t : t + 2], axis=0).astype(jnp.bfloat16)
         return carry
 
-    lax.fori_loop(0, HALF // 128, one, 0, unroll=2)
+    lax.fori_loop(0, HALF // 128, one, 0, unroll=4)
 
 
 def own_kernel(core_ref, own_hbm, window_hbm, table_hbm, u_ref, v_ref, frames_ref, window_ref, table_ref, own_ref, sems):

time: 81.5 us -> 81.3 us (level)
  no operation moved by 1% of the time
where the time goes in v7:
time: 81.3 us; the launch traced here: 81.2 us
  waiting for transfers between devices  44.3 us (54%)
  starting transfers between devices  26.4 us (32%)
  Pallas kernels  9.68 us (12%)
    all_to_all x1, waiting for transfers between devices, shards(): lax.all_to_all(messages.reshape(N_FREQ * N_BLK, 3, 2, 128), ('core', 'z_h...  44.3 us
    all_to_all x1, starting transfers between devices, shards(): lax.all_to_all(messages.reshape(N_FREQ * N_BLK, 3, 2, 128), ('core', 'z_h...  17.5 us
    ppermute x1, starting transfers between devices, shards(): other = lax.ppermute(samples, 'core', [(0, 1), (1, 0)])  8.91 us
    pallas_call x1, Pallas kernels, visibility_tiles(): pl.pallas_call(correlate_kernel, grid=(2,), in_specs=[pl.BlockSpec(memory...  4.02 us
    pallas_call x1, Pallas kernels, channel_messages(): pl.pallas_call(channel_kernel, in_specs=[pl.BlockSpec(memory_space=pltpu....  3.23 us
    pallas_call x1, Pallas kernels, own_part(): pl.pallas_call(own_kernel, in_specs=[pl.BlockSpec(memory_space=pltpu.SMEM...  2.43 us
  transfers between devices with their start and end apart: 2, of which 1 were waited for; matrix products, arithmetic and copies ran while one was open for 0% of the time, Pallas kernels for 3%

profile of v7, /device:TPU:1, one launch (start us, length us, event | category | flops | bytes accessed | tf_op | source)
XLA Modules:
  0.0 81.2 jit_solution(9712668300740801035)
XLA Ops:
  0.0 0.0 copy-start.1
  0.0 8.9 %collective-permute-start = (bf16[8,16,2048]{2,1,0:T(8,128)(2,1)}, bf16[8,16,2048]{2,1,0:T(8,128)(2,1)S(1)}, u32[]{:S(2)}, u32[]{:S(2)}) collective-permute-start(bf16[8,16,2048]{2,1,0:T(8,128)(2,1)} %own_hbm.1), channel_id=1, source_target_pairs={{0,1},{1,0},{2,3},{3,2},{4,5},{5,4},{6,7},{7,6},{8,9},{9,8},{10,11... | collective-permute-start | bytes 1572872 | tf_op jit(solution)/shard_map/ppermute | solution.py:351
  8.9 2.4 %own.1 = (bf16[128,1024]{1,0:T(8,128)(2,1)S(1)}, bf16[128,1024]{1,0:T(8,128)(2,1)S(1)}, f32[2048,128]{1,0:T(8,128)S(1)}, f32[16,2048]{1,0:T(8,128)S(1)}, bf16[4,2,256,1024]{3,2,1,0:T(8,128)(2,1)S(1)}) custom-call(s32[1]{0:T(128)} %bitcast.core_ref, bf16[8,16,2048]{2,1,0:T(8,128)(2,1)} %own_hbm.1, f32[16,2048]{1,0:T(8,128)} %constant.10.clone.window_hbm, ...), custom_call_target="tpu_custom_call" | custom-call | flops 10000000 | bytes 2000000 | tf_op jit(solution)/shard_map/own/pallas_call | solution.py:219
  11.4 0.0 collective-permute-done.other_ref
  11.4 0.0 copy-done.1
  11.4 0.0 copy-start
  11.4 3.2 %channels.1 = bf16[3072,128]{1,0:T(8,128)(2,1)} custom-call(s32[1]{0:T(128)} %bitcast.core_ref, f32[2048,128]{1,0:T(8,128)S(1)} %get-tuple-element.10.frames_ref, bf16[8,16,2048]{2,1,0:T(8,128)(2,1)S(1)} %collective-permute-done.other_ref, f32[16,2048]{1,0:T(8,128)S(1)} %get-tuple-element.11.window_ref, ...), custom_call_target="tpu_custom_call" | custom-call | tf_op jit(solution)/shard_map/channels/pallas_call | solution.py:242
  14.6 17.5 %all-to-all-start = ((bf16[512,3,2,128]{3,2,1,0:T(2,128)(2,1)}), bf16[512,3,2,128]{3,2,1,0:T(2,128)(2,1)S(1)}, u32[]{:S(2)}, u32[]{:S(2)}) async-start(bf16[512,3,2,128]{3,2,1,0:T(2,128)(2,1)} %bitcast.2), calls=%async_computation | async-start | bytes 1572864 | tf_op jit(solution)/shard_map/all_to_all | solution.py:354
  32.8 44.3 %all-to-all-done = bf16[512,3,2,128]{3,2,1,0:T(2,128)(2,1)S(1)} async-done(((bf16[512,3,2,128]{3,2,1,0:T(2,128)(2,1)}), bf16[512,3,2,128]{3,2,1,0:T(2,128)(2,1)S(1)}, u32[]{:S(2)}, u32[]{:S(2)}) %all-to-all-start) | async-done | bytes 786464 | tf_op jit(solution)/shard_map/all_to_all | solution.py:354
  77.2 0.0 copy-done
  77.2 4.0 %correlate.1 = bf16[2,136,64,128]{3,2,1,0:T(8,128)(2,1)} custom-call(s32[1,1]{1,0:T(1,128)S(6)} %copy.8.count_ref, bf16[3072,128]{1,0:T(8,128)(2,1)S(1)} %bitcast.9, bf16[4096,256]{1,0:T(8,128)(2,1)S(1)} %copy-done), custom_call_target="tpu_custom_call" | custom-call | tf_op jit(solution)/shard_map/correlate/pallas_call | solution.py:326
Async XLA Ops:
  0.0 11.4 %copy-start.1 = (s32[4,128,2]{1,2,0:T(2,128)S(1)}, s32[4,128,2]{1,2,0:T(2,128)}, u32[]{:S(2)}) copy-start(s32[4,128,2]{1,2,0:T(2,128)} %param.7) | copy-start | bytes 12292
  0.0 11.4 %collective-permute-start = (bf16[8,16,2048]{2,1,0:T(8,128)(2,1)}, bf16[8,16,2048]{2,1,0:T(8,128)(2,1)S(1)}, u32[]{:S(2)}, u32[]{:S(2)}) collective-permute-start(bf16[8,16,2048]{2,1,0:T(8,128)(2,1)} %own_hbm.1), channel_id=1, source_target_pairs={{0,1},{1,0},{2,3},{3,2},{4,5},{5,4},{6,7},{7,6},{8,9},{9,8},{10,11... | collective-permute-start | bytes 1572872 | tf_op jit(solution)/shard_map/ppermute | solution.py:351
  11.4 65.8 %copy-start = (bf16[4096,256]{1,0:T(8,128)(2,1)S(1)}, bf16[4096,256]{1,0:T(8,128)(2,1)}, u32[]{:S(2)}) copy-start(bf16[4096,256]{1,0:T(8,128)(2,1)} %constant.12.clone.merge_ref) | copy-start | bytes 6291460
  14.6 62.5 %all-to-all-start = ((bf16[512,3,2,128]{3,2,1,0:T(2,128)(2,1)}), bf16[512,3,2,128]{3,2,1,0:T(2,128)(2,1)S(1)}, u32[]{:S(2)}, u32[]{:S(2)}) async-start(bf16[512,3,2,128]{3,2,1,0:T(2,128)(2,1)} %bitcast.2), calls=%async_computation | async-start | bytes 1572864 | tf_op jit(solution)/shard_map/all_to_all | solution.py:354
